TPU v7x, 256 devices: a whole 4x4x8 slice. The times are simulated.
256 devices in a mesh: grid: 8 (over y, core), mesh: 32 (over x, z).
Axes of the slice: x: 4, y: 4, z: 8, core: 2. Of those that a mesh axis runs over, the one named last changes fastest.
Arguments:
- grid_feats: bfloat16 [131072, 227], P(('grid', 'mesh')), may hold values from -6 to 6
- g2m_src: int32 [768, 256], P(('grid', 'mesh')), may hold values from 0 to 511
- g2m_count: int32 [256, 3], P(('grid', 'mesh')), may hold values from 32 to 256, as said below
- g2m_dst: int32 [768, 256], P(('grid', 'mesh')), may hold values from 0 to 63
- g2m_weight: bfloat16 [768, 256], P(('grid', 'mesh')), may hold values from 0.29882812 to 3
- halo_send: int32 [8192, 16], P(('grid', 'mesh')), may hold values from 0 to 63
- mesh_src: int32 [16384, 6], P(('grid', 'mesh')), may hold values from 0 to 575
- cotangent: bfloat16 [16384, 512], P(('grid', 'mesh')), may hold values from -24 to 24
- w_embed: bfloat16 [227, 512], replicated, may hold values from -0.375 to 0.375
- w_encode: bfloat16 [2, 512, 512], replicated, may hold values from -0.25 to 0.25
- w_layers: bfloat16 [2, 3, 512, 512], replicated, may hold values from -0.25 to 0.25
- gains: float32 [4, 512], replicated, may hold values from 0.5 to 1.5
Outputs:
- mesh_out: bfloat16 [16384, 512], P(('grid', 'mesh'))
- grad_layers: float32 [2, 3, 512, 512], P(None, None, None, 'mesh')
- grad_encoder: float32 [2, 512, 512], P(None, None, 'mesh')
- grad_embed: float32 [227, 512], replicated
Inputs may be any that keep to these rules, and one draw needn't show every extreme that they name: `g2m_count`: multiples of 32; slots are used from slot 0 on; in every band some sector receives all 256 slots from each of its three sources. `mesh_src`: rows below 64 are the sector's own nodes; row 64 + m * 16 + k is the k-th row copied from sector m of the band.
All inputs are finite; a program needn't handle non-finite values.
Results may differ from a plain program's by a relative error of at most 0.03.
Values may be sent and summed in bfloat16 or wider, within the bound.
No kernel may reach another device: no remote copies, remote signals or barrier semaphores. Data moves between devices by JAX's collectives and lax.ppermute only.
A program may use at most 128 MiB of HBM per device.

v0:
```python
import math

import jax
import jax.numpy as jnp
from jax import lax
from jax.experimental import pallas as pl
from jax.experimental.pallas import tpu as pltpu
from jax.sharding import PartitionSpec as P

NORM_EPSILON = 1e-05
BF16 = jnp.bfloat16
F32 = jnp.float32


def side_pairs(count):
    forward = [(i, (i + 1) % count) for i in range(count)]
    backward = [((i + 1) % count, i) for i in range(count)]
    return forward, backward


def from_sides(to_east, to_west):
    forward, backward = side_pairs(lax.axis_size("mesh"))
    return lax.ppermute(to_east, "mesh", forward), lax.ppermute(to_west, "mesh", backward)


def exchange(blocks, axis):
    return lax.all_to_all(blocks, axis, split_axis=0, concat_axis=0, tiled=True)


def spread(block, axis):
    count = lax.axis_size(axis)
    return exchange(jnp.broadcast_to(block[None], (count,) + block.shape), axis)


def along_y(block, step):
    count = lax.axis_size("grid")
    return lax.ppermute(block, "grid", [(i, (i + 2 * step) % count) for i in range(count)])


def to_other_core(block):
    return lax.ppermute(block, "grid", [(i, i ^ 1) for i in range(lax.axis_size("grid"))])


def normalize(values):
    average = jnp.mean(values, axis=-1, keepdims=True)
    centred = values - average
    inverse = lax.rsqrt(jnp.mean(centred * centred, axis=-1, keepdims=True) + NORM_EPSILON)
    return (centred * inverse, inverse)


def normalize_back(grad_hat, normed, inverse):
    first = jnp.mean(grad_hat, axis=-1, keepdims=True)
    second = jnp.mean(grad_hat * normed, axis=-1, keepdims=True)
    return inverse * (grad_hat - first - normed * second)


def silu(values):
    return values * jax.nn.sigmoid(values)


def silu_slope(values):
    logistic = jax.nn.sigmoid(values)
    return logistic * (1.0 + values * (1.0 - logistic))


def matmul(matrix_a, matrix_b):
    return jnp.dot(matrix_a, matrix_b, preferred_element_type=F32)


def left_transposed(matrix_a, matrix_b):
    return lax.dot_general(
        matrix_a, matrix_b, (((0,), (0,)), ((), ())), preferred_element_type=F32
    )


def right_transposed(matrix_a, matrix_b):
    return lax.dot_general(
        matrix_a, matrix_b, (((1,), (1,)), ((), ())), preferred_element_type=F32
    )


def hits(index_row, count):
    rows = lax.broadcasted_iota(jnp.int32, (count, index_row.shape[1]), 0)
    return jnp.where(rows == index_row, 1.0, 0.0).astype(BF16)


def weighted_hits(info, count):
    rows = lax.broadcasted_iota(jnp.int32, (count, info.shape[1]), 0).astype(F32)
    return jnp.where(rows == info[0:1], info[1:2], 0.0).astype(BF16)


def live_hits(index_row, live, count):
    shape = (count, index_row.shape[1])
    rows = lax.broadcasted_iota(jnp.int32, shape, 0)
    slots = lax.broadcasted_iota(jnp.int32, shape, 1)
    return jnp.where((rows == index_row) & (slots < live), 1.0, 0.0).astype(BF16)


def call(kernel, outs, args, flops, scalars=(), picked=None):
    picked = picked or {}
    specs = []
    for place, arg in enumerate(args):
        if place in scalars:
            specs.append(pl.BlockSpec(memory_space=pltpu.SMEM))
        elif place in picked:
            lead, zeros = picked[place], (0,) * (arg.ndim - 1)
            specs.append(
                pl.BlockSpec((None,) + arg.shape[1:], lambda i, lead=lead, zeros=zeros: (lead,) + zeros)
            )
        else:
            specs.append(pl.BlockSpec(arg.shape, lambda i, zeros=(0,) * arg.ndim: zeros))
    shapes = [jax.ShapeDtypeStruct(shape, dtype) for shape, dtype in outs]
    moved = sum(math.prod(s.shape) * s.dtype.itemsize for s in list(args) + shapes)
    return pl.pallas_call(
        kernel,
        grid=(1,),
        in_specs=specs,
        out_specs=[
            pl.BlockSpec(s.shape, lambda i, zeros=(0,) * len(s.shape): zeros) for s in shapes
        ],
        out_shape=shapes,
        compiler_params=pltpu.CompilerParams(vmem_limit_bytes=60 * 2**20),
        cost_estimate=pl.CostEstimate(flops=flops, bytes_accessed=moved, transcendentals=0),
    )(*args)


def edge_forward(counts, feats, sources, w_embed, w_edge, gains, pre_out, rows_out, edge_out, message_out):
    grid_pre = left_transposed(feats[...], w_embed[...])
    pre_out[...] = grid_pre
    normed, _ = normalize(silu(grid_pre))
    latent = (normed * gains[0:1]).astype(BF16)
    slots = sources.shape[1]
    for side in range(3):
        chosen = live_hits(sources[side : side + 1], counts[0, side], latent.shape[0])
        rows = left_transposed(chosen, latent).astype(BF16)
        edge_pre = matmul(rows, w_edge[...])
        place = pl.ds(side * slots, slots)
        rows_out[place] = rows
        edge_out[place] = edge_pre
        message_out[place] = silu(edge_pre).astype(BF16)


def edge_sums(info_west, info_own, info_east, messages, west_out, own_out, east_out):
    nodes = own_out.shape[0]
    slots = info_own.shape[1]
    sides = ((info_west, west_out), (info_own, own_out), (info_east, east_out))
    for side, (info, out) in enumerate(sides):
        total = matmul(weighted_hits(info[...], nodes), messages[pl.ds(side * slots, slots)])
        out[...] = total.astype(out.dtype)


def mesh_start(own, west, east, w_node, gains, sends, sum_out, latent_out, sent_out):
    mesh_sum = (own[...] + west[...].astype(F32) + east[...].astype(F32)).astype(BF16)
    sum_out[...] = mesh_sum
    normed, _ = normalize(matmul(mesh_sum, w_node[...]))
    latent = (normed * gains[1:2]).astype(BF16)
    latent_out[...] = latent
    sent_out[...] = left_transposed(hits(sends[...], latent.shape[0]), latent).astype(BF16)


def layer_values(latent, halo, links, weights, degree):
    nodes, width = latent.shape
    own = left_transposed(hits(links, nodes), latent)
    far = left_transposed(hits(links - nodes, halo.shape[0]), halo)
    gathered = (own + far).astype(BF16)
    pair_pre = matmul(gathered, weights[0]).reshape(degree, nodes, width) + matmul(latent, weights[1])[None]
    message = silu(pair_pre).astype(BF16)
    node_sum = jnp.sum(message.astype(F32), axis=0).astype(BF16)
    return gathered, pair_pre, node_sum, matmul(node_sum, weights[2])


def layer_back(upstream, gain, gathered, pair_pre, node_out, links, weights, halo_rows):
    degree, nodes, width = pair_pre.shape
    normed, inverse = normalize(node_out)
    grad_norm = normalize_back(upstream * gain, normed, inverse).astype(BF16)
    grad_node = right_transposed(grad_norm, weights[2])
    grad_pair_pre = grad_node[None] * silu_slope(pair_pre)
    grad_pair = grad_pair_pre.astype(BF16).reshape(degree * nodes, width)
    grad_self = jnp.sum(grad_pair_pre, axis=0).astype(BF16)
    grad_rows = right_transposed(grad_pair, weights[0]).astype(BF16)
    grad_halo = matmul(hits(links - nodes, halo_rows), grad_rows)
    upstream = upstream + right_transposed(grad_self, weights[1]) + matmul(hits(links, nodes), grad_rows)
    return grad_norm, grad_pair, grad_self, grad_halo.astype(BF16), upstream


def layer_forward(
    latent, halo, links, weights, gains, sends, gathered_out, pair_out, sum_out, node_out, latent_out, sent_out
):
    nodes = latent.shape[0]
    gathered, pair_pre, node_sum, node_pre = layer_values(
        latent[...], halo[...], links[...], weights, pair_out.shape[0]
    )
    normed, _ = normalize(node_pre)
    after = (latent[...].astype(F32) + normed * gains[2:3]).astype(BF16)
    latent_out[...] = after
    sent_out[...] = left_transposed(hits(sends[...], nodes), after).astype(BF16)
    gathered_out[...] = gathered
    pair_out[...] = pair_pre
    sum_out[...] = node_sum
    node_out[...] = node_pre


def layer_last(
    scale,
    latent,
    halo,
    links,
    weights,
    gains,
    cotangent,
    latent_out,
    gathered_out,
    sum_out,
    norm_out,
    pair_out,
    self_out,
    halo_out,
    up_out,
):
    nodes = latent.shape[0]
    gathered, pair_pre, node_sum, node_pre = layer_values(
        latent[...], halo[...], links[...], weights, links.shape[1] // nodes
    )
    normed, _ = normalize(node_pre)
    latent_out[...] = (latent[...].astype(F32) + normed * gains[3:4]).astype(BF16)
    gathered_out[...] = gathered
    sum_out[...] = node_sum
    upstream = cotangent[...].astype(F32) * scale
    norm_out[...], pair_out[...], self_out[...], halo_out[...], up_out[...] = layer_back(
        upstream, gains[3:4], gathered, pair_pre, node_pre, links[...], weights, halo.shape[0]
    )


def layer_first_back(
    upstream,
    returned,
    sends,
    gathered,
    pair_pre,
    node_pre,
    links,
    weights,
    gains,
    norm_out,
    pair_out,
    self_out,
    halo_out,
    up_out,
):
    nodes = upstream.shape[0]
    total = upstream[...] + matmul(hits(sends[...], nodes), returned[...])
    norm_out[...], pair_out[...], self_out[...], halo_out[...], up_out[...] = layer_back(
        total, gains[2:3], gathered[...], pair_pre[...], node_pre[...], links[...], weights, returned.shape[0]
    )


def weight_grads(core, gathered, grad_pair, latent, grad_self, node_sum, grad_norm, kept, sent):
    blocks, _, rows, width = kept.shape
    pairs = ((gathered, grad_pair), (latent, grad_self), (node_sum, grad_norm))
    for place, (rows_in, grads) in enumerate(pairs):
        total = left_transposed(rows_in[...], grads[...]).reshape(blocks, 2, rows, width)
        first = core[0] == 0
        kept[:, place] = jnp.where(first, total[:, 0], total[:, 1]).astype(BF16)
        sent[:, place] = jnp.where(first, total[:, 1], total[:, 0]).astype(BF16)


def add_cores(chip, last_kept, last_other, first_kept, first_other, *outs):
    blocks, rows, _ = last_kept.shape
    pairs = ((last_kept, last_other), (first_kept, first_other))
    for step, out in enumerate(outs):
        place = lax.rem(chip[0] + step, blocks)
        for layer, (kept, other) in enumerate(pairs):
            total = kept[place].astype(F32) + other[place].astype(F32)
            out[pl.ds(layer * rows, rows)] = total.astype(BF16)


def start_back(upstream, returned, sends, mesh_sum, w_node, gains, start_out, sum_out):
    nodes = upstream.shape[0]
    total = upstream[...] + matmul(hits(sends[...], nodes), returned[...])
    normed, inverse = normalize(matmul(mesh_sum[...], w_node[...]))
    grad_start = normalize_back(total * gains[1:2], normed, inverse).astype(BF16)
    start_out[...] = grad_start
    sum_out[...] = right_transposed(grad_start, w_node[...]).astype(BF16)


def edge_back(
    counts,
    core,
    info_west,
    info_own,
    info_east,
    grad_west,
    grad_own,
    grad_east,
    edge_pre,
    edge_rows,
    grid_pre,
    feats,
    sources,
    w_edge,
    gains,
    mesh_sum,
    grad_start,
    kept_out,
    sent_out,
):
    slots = sources.shape[1]
    nodes = grad_own.shape[0]
    channels, grid_nodes = feats.shape
    width = grid_pre.shape[1]
    half = width // 2
    grad_grid = jnp.zeros((grid_nodes, width), F32)
    edge_w = jnp.zeros((width, width), F32)
    sides = ((info_west, grad_west), (info_own, grad_own), (info_east, grad_east))
    for side, (info, grads) in enumerate(sides):
        place = pl.ds(side * slots, slots)
        grad_message = left_transposed(weighted_hits(info[...], nodes), grads[...]).astype(BF16)
        grad_edge = (grad_message.astype(F32) * silu_slope(edge_pre[place])).astype(BF16)
        edge_w += left_transposed(grad_edge, edge_rows[place])
        grad_rows = right_transposed(grad_edge, w_edge[...]).astype(BF16)
        chosen = live_hits(sources[side : side + 1], counts[0, side], grid_nodes)
        grad_grid += matmul(chosen, grad_rows)
    node_w = left_transposed(grad_start[...], mesh_sum[...])
    values = grid_pre[...]
    normed, inverse = normalize(silu(values))
    grad_act = (normalize_back(grad_grid * gains[0:1], normed, inverse) * silu_slope(values)).astype(BF16)
    embed = matmul(feats[...], grad_act)
    spare = 2 * EMBED_HALF - channels
    embed = jnp.concatenate([embed, jnp.zeros((spare, width), F32)], axis=0).T
    low = jnp.concatenate([edge_w[:, :half], node_w[:, :half], embed[:, :EMBED_HALF]], axis=1).astype(BF16)
    high = jnp.concatenate([edge_w[:, half:], node_w[:, half:], embed[:, EMBED_HALF:]], axis=1).astype(BF16)

    @pl.when(core[0] == 0)
    def _():
        kept_out[...] = low
        sent_out[...] = high

    @pl.when(core[0] != 0)
    def _():
        kept_out[...] = high
        sent_out[...] = low


EMBED_HALF = 128


def pack(kept, other, *refs):
    blocks, out = refs[:-1], refs[-1]
    rows = blocks[0].shape[0]
    total = sum(block[...].astype(F32) for block in blocks)
    out[:, :rows] = total.T.astype(BF16)
    out[:, rows:] = (kept[...].astype(F32) + other[...].astype(F32)).astype(BF16)


def sum_blocks(blocks, out):
    total = jnp.sum(blocks[...].astype(F32), axis=0).astype(BF16)
    out[...] = jnp.broadcast_to(total[None], out.shape)


def local(
    grid_feats,
    g2m_src,
    g2m_count,
    g2m_dst,
    g2m_weight,
    halo_send,
    mesh_src,
    cotangent,
    w_embed,
    w_encode,
    w_layers,
    gains,
):
    peers = lax.axis_size("mesh")
    bands = lax.axis_size("grid")
    nodes, degree = mesh_src.shape
    grid_nodes, channels = grid_feats.shape
    width = w_embed.shape[1]
    slots = g2m_src.shape[1]
    halo_rows = halo_send.size
    columns = width // peers
    pairs = nodes * degree
    layers = w_layers.shape[0]
    unit = 2 * width * width
    band = lax.axis_index("grid").astype(jnp.int32)
    core = (band % 2).reshape(1)
    chip = (band // 2).reshape(1)
    sends = halo_send.reshape(1, -1)
    links = mesh_src.T.reshape(1, -1)
    feats = grid_feats.T

    edge_info = jnp.stack([g2m_dst.astype(F32), g2m_weight.astype(F32)], axis=1)
    info_west, info_east = from_sides(edge_info[2], edge_info[0])
    info = [info_west, edge_info[1], info_east]
    grid_pre, edge_rows, edge_pre, messages = call(
        edge_forward,
        [
            ((grid_nodes, width), F32),
            ((3 * slots, width), BF16),
            ((3 * slots, width), F32),
            ((3 * slots, width), BF16),
        ],
        [g2m_count, feats, g2m_src, w_embed, w_encode, gains],
        unit * 8 * slots,
        scalars=(0,),
        picked={4: 0},
    )
    sum_west, sum_own, sum_east = call(
        edge_sums,
        [((nodes, width), BF16), ((nodes, width), F32), ((nodes, width), BF16)],
        [*info, messages],
        unit * slots,
    )
    got_west, got_east = from_sides(sum_east, sum_west)
    mesh_sum, latent, sent = call(
        mesh_start,
        [((nodes, width), BF16), ((nodes, width), BF16), ((halo_rows, width), BF16)],
        [sum_own, got_west, got_east, w_encode, gains, sends],
        unit * nodes * 2,
        picked={3: 1},
    )
    halo = exchange(sent.reshape(peers, -1, width), "mesh").reshape(-1, width)
    gathered, pair_pre, node_sum, node_pre, middle, sent = call(
        layer_forward,
        [
            ((pairs, width), BF16),
            ((degree, nodes, width), F32),
            ((nodes, width), BF16),
            ((nodes, width), F32),
            ((nodes, width), BF16),
            ((halo_rows, width), BF16),
        ],
        [latent, halo, links, w_layers, gains, sends],
        unit * pairs * 2,
        picked={3: 0},
    )
    halo = exchange(sent.reshape(peers, -1, width), "mesh").reshape(-1, width)
    loss_scale = jnp.full((1,), 1.0 / math.sqrt(nodes * bands * peers), F32)
    back_shapes = [
        ((nodes, width), BF16),
        ((pairs, width), BF16),
        ((nodes, width), BF16),
        ((halo_rows, width), BF16),
        ((nodes, width), F32),
    ]

    def core_halves(*arrays):
        shape = (bands // 2, 3, width // bands, width)
        kept, sent = call(
            weight_grads, [(shape, BF16)] * 2, [core, *arrays], unit * (pairs + 2 * nodes), scalars=(0,)
        )
        rows = (bands // 2, 3 * width // bands, width)
        return kept.reshape(rows), to_other_core(sent).reshape(rows)

    def last_layer(scale, *refs):
        layer_last(scale[0], *refs)

    mesh_out, last_gathered, last_sum, last_norm, last_pair, last_self, grad_halo, upstream = call(
        last_layer,
        [((nodes, width), BF16), ((pairs, width), BF16), ((nodes, width), BF16)] + back_shapes,
        [loss_scale, middle, halo, links, w_layers, gains, cotangent],
        unit * pairs * 4,
        scalars=(0,),
        picked={4: 1},
    )
    returned = exchange(grad_halo.reshape(peers, -1, width), "mesh").reshape(-1, width)
    last_rows = core_halves(last_gathered, last_pair, middle, last_self, last_sum, last_norm)
    returned, last_rows = lax.optimization_barrier((returned, last_rows))
    grad_norm, grad_pair, grad_self, grad_halo, upstream = call(
        layer_first_back,
        back_shapes,
        [upstream, returned, sends, gathered, pair_pre, node_pre, links, w_layers, gains],
        unit * pairs * 3,
        picked={7: 0},
    )
    returned = exchange(grad_halo.reshape(peers, -1, width), "mesh").reshape(-1, width)
    first_rows = core_halves(gathered, grad_pair, latent, grad_self, node_sum, grad_norm)
    chips = bands // 2
    shared = 6 * width // bands
    parts = call(
        add_cores, [((shared, width), BF16)] * chips, [chip, *last_rows, *first_rows], 0, scalars=(0,)
    )
    returned, parts = lax.optimization_barrier((returned, parts))
    grad_start, grad_sum = call(
        start_back,
        [((nodes, width), BF16), ((nodes, width), BF16)],
        [upstream, returned, sends, mesh_sum, w_encode, gains],
        unit * nodes * 3,
        picked={4: 1},
    )
    grad_west, grad_east = from_sides(grad_sum, grad_sum)
    grad_sum, parts = lax.optimization_barrier((grad_sum, parts))
    parts = [parts[0]] + [along_y(parts[step], step) for step in range(1, chips)]
    part = width + EMBED_HALF
    kept, passed = call(
        edge_back,
        [((width, part), BF16), ((width, part), BF16)],
        [
            g2m_count,
            core,
            *info,
            grad_west,
            grad_sum,
            grad_east,
            edge_pre,
            edge_rows,
            grid_pre,
            feats,
            g2m_src,
            w_encode,
            gains,
            mesh_sum,
            grad_start,
        ],
        unit * 12 * slots,
        scalars=(0, 1),
        picked={13: 0},
    )
    kept, passed, parts = lax.optimization_barrier((kept, passed, parts))
    other = to_other_core(passed)
    (packed,) = call(
        pack, [((width, shared + part), BF16)], [kept, other, *parts], 0
    )
    arrived = exchange(packed.reshape(peers, columns, -1), "mesh")
    (summed,) = call(sum_blocks, [((bands, columns, shared + part), BF16)], [arrived], 0)
    held = exchange(summed, "grid")
    tail = held[:, :, shared:].reshape(bands // 2, 2, columns, part).astype(F32)
    tail = jnp.sum(tail, axis=0)
    half = width // 2
    embed = jnp.concatenate([tail[0, :, width:], tail[1, :, width:]], axis=1)
    embed = spread(embed.astype(BF16), "mesh")
    total_embed = embed.reshape(width, -1).T[:channels].astype(F32)
    edge_w = jnp.concatenate([tail[0, :, :half], tail[1, :, :half]], axis=1).T
    node_w = jnp.concatenate([tail[0, :, half:width], tail[1, :, half:width]], axis=1).T
    whole = held[:, :, :shared].reshape(bands, columns, layers, 3, width // bands)
    whole = whole[:, :, ::-1].transpose(2, 3, 1, 0, 4).reshape(layers, 3, columns, width).swapaxes(2, 3)
    return mesh_out, whole.astype(F32), jnp.stack([edge_w, node_w]), total_embed


def solution(mesh):
    placed = (P(("grid", "mesh"), None),) * 8 + (P(),) * 4
    return jax.shard_map(
        local,
        mesh=mesh,
        in_specs=placed,
        out_specs=(
            P(("grid", "mesh"), None),
            P(None, None, None, "mesh"),
            P(None, None, "mesh"),
            P(),
        ),
        check_vma=False,
    )
```

profile of v0, /device:TPU:32, one launch (start us, length us, event | category | flops | bytes accessed | tf_op | source)
XLA Modules:
  0.0 223.1 jit_solution(17614641127834762400)
XLA Ops:
  4.7 4.5 %shard_map.147 = (f32[512,512]{1,0:T(8,128)}, bf16[768,512]{1,0:T(8,128)(2,1)}, f32[768,512]{1,0:T(8,128)}, bf16[768,512]{1,0:T(8,128)(2,1)}) custom-call(s32[1,3]{1,0:T(1,128)} %counts.3, bf16[227,512]{1,0:T(8,128)(2,1)} %bitcast.70, s32[3,256]{1,0:T(4,128)} %sources.3, bf16[227,512]{1,0:T(8,128)(2,1)} %w_embed.1, bf16[2,512,512]{2,1,0:T(8,128)(2,1)} %w_edge.3, ...), custom_call_target="tpu_custom_call" | custom-call | flops 1073741824 | bytes 5719052 | tf_op jit(solution)/shard_map/pallas_call | solution.py:114
  9.2 3.2 %collective-permute-done.info_west = f32[2,256]{1,0:T(2,128)S(1)} collective-permute-done((f32[2,256]{1,0:T(2,128)S(1)}, f32[2,256]{1,0:T(2,128)S(1)}, u32[]{:S(2)}, u32[]{:S(2)}) %collective-permute-start) | collective-permute-done | bytes 2080 | tf_op jit(solution)/shard_map/ppermute | solution.py:23
  15.0 5.3 %collective-permute-start.3 = (bf16[64,512]{1,0:T(8,128)(2,1)}, bf16[64,512]{1,0:T(8,128)(2,1)S(1)}, u32[]{:S(2)}, u32[]{:S(2)}) collective-permute-start(bf16[64,512]{1,0:T(8,128)(2,1)} %get-tuple-element.67), channel_id=1, source_target_pairs={{1,0},{2,1},{3,2},{4,3},{5,4},{6,5},{7,6},{8,7},{9,8},{10,9},{11,1... | collective-permute-start | bytes 196616 | tf_op jit(solution)/shard_map/ppermute | solution.py:23
  26.0 12.1 %all-to-all-start = ((bf16[32,16,512]{2,1,0:T(8,128)(2,1)}), bf16[32,16,512]{2,1,0:T(8,128)(2,1)S(1)}, u32[]{:S(2)}, u32[]{:S(2)}) async-start(bf16[32,16,512]{2,1,0:T(8,128)(2,1)} %bitcast.66), calls=%async_computation | async-start | bytes 1048576 | tf_op jit(solution)/shard_map/all_to_all | solution.py:27
  38.7 14.3 %all-to-all-done = bf16[32,16,512]{2,1,0:T(8,128)(2,1)S(1)} async-done(((bf16[32,16,512]{2,1,0:T(8,128)(2,1)}), bf16[32,16,512]{2,1,0:T(8,128)(2,1)S(1)}, u32[]{:S(2)}, u32[]{:S(2)}) %all-to-all-start) | async-done | bytes 524320 | tf_op jit(solution)/shard_map/all_to_all | solution.py:27
  53.8 4.0 %shard_map.150 = (bf16[384,512]{1,0:T(8,128)(2,1)}, f32[6,64,512]{2,1,0:T(8,128)}, bf16[64,512]{1,0:T(8,128)(2,1)}, f32[64,512]{1,0:T(8,128)}, bf16[64,512]{1,0:T(8,128)(2,1)}, /*index=5*/bf16[512,512]{1,0:T(8,128)(2,1)}) custom-call(bf16[64,512]{1,0:T(8,128)(2,1)} %get-tuple-element.68.latent, bf16[512,512]{1,0:T(8,128)(2,1)} %bitcast.56, ...), custom_call_target="tpu_custom_call" | custom-call | flops 402653184 | bytes 5713408 | tf_op jit(solution)/shard_map/pallas_call | solution.py:114
  57.8 19.1 %all_to_all.35 = bf16[32,16,512]{2,1,0:T(8,128)(2,1)} all-to-all(bf16[32,16,512]{2,1,0:T(8,128)(2,1)} %bitcast.67), channel_id=1, replica_groups=mesh['grid'=8,'mesh'=32] {'mesh'}, dimensions={0} | all-to-all | bytes 1048576 | tf_op jit(solution)/shard_map/all_to_all | solution.py:27
  76.9 4.7 %shard_map.151 = (bf16[64,512]{1,0:T(8,128)(2,1)}, bf16[384,512]{1,0:T(8,128)(2,1)}, bf16[64,512]{1,0:T(8,128)(2,1)}, bf16[64,512]{1,0:T(8,128)(2,1)}, bf16[384,...) custom-call(f32[1]{0:T(128)} %constant.26.clone.1.scale, ...), custom_call_target="tpu_custom_call" | custom-call | flops 805306368 | bytes 5514756 | tf_op jit(solution)/shard_map/pallas_call | solution.py:114
  81.6 4.4 %all-to-all-start.2 = ((bf16[32,16,512]{2,1,0:T(8,128)(2,1)}), bf16[32,16,512]{2,1,0:T(8,128)(2,1)S(1)}, u32[]{:S(2)}, u32[]{:S(2)}) async-start(bf16[32,16,512]{2,1,0:T(8,128)(2,1)} %bitcast.65), calls=%async_computation.2 | async-start | bytes 1048576 | tf_op jit(solution)/shard_map/all_to_all | solution.py:27
  86.1 3.1 %shard_map.152 = (bf16[4,3,64,512]{3,2,1,0:T(8,128)(2,1)}, bf16[4,3,64,512]{3,2,1,0:T(8,128)(2,1)}) custom-call(s32[1]{0:T(128)} %bitcast.9.core, bf16[384,512]{1,0:T(8,128)(2,1)} %get-tuple-element.75.gathered, bf16[384,512]{1,0:T(8,128)(2,1)} %get-tuple-element.76.grad_pair, bf16[64,512]{1,0:T(8,128)(2,1)} %get-tuple-element.70.refs_0_.latent, ...), custom_call_target="tpu_custom_call" | custom-call | flops 268435456 | bytes 2621444 | tf_op jit(solution)/shard_map/pallas_call | solution.py:114
  91.6 8.4 %all-to-all-done.2 = bf16[32,16,512]{2,1,0:T(8,128)(2,1)S(1)} async-done(((bf16[32,16,512]{2,1,0:T(8,128)(2,1)}), bf16[32,16,512]{2,1,0:T(8,128)(2,1)S(1)}, u32[]{:S(2)}, u32[]{:S(2)}) %all-to-all-start.2) | async-done | bytes 524320 | tf_op jit(solution)/shard_map/all_to_all | solution.py:27
  100.8 4.1 %shard_map.153 = (bf16[64,512]{1,0:T(8,128)(2,1)}, bf16[384,512]{1,0:T(8,128)(2,1)}, bf16[64,512]{1,0:T(8,128)(2,1)}, bf16[512,512]{1,0:T(8,128)(2,1)}, f32[64,512]{1,0:T(8,128)}) custom-call(f32[64,512]{1,0:T(8,128)} %get-tuple-element.73.upstream, bf16[512,512]{1,0:T(8,128)(2,1)} %bitcast.57, s32[1,512]{1,0:T(1,128)} %reshape.88.sends, ...), custom_call_target="tpu_custom_call" | custom-call | flops 603979776 | bytes 6303232 | tf_op jit(solution)/shard_map/pallas_call | solution.py:114
  104.9 4.4 %all-to-all-start.3 = ((bf16[32,16,512]{2,1,0:T(8,128)(2,1)}), bf16[32,16,512]{2,1,0:T(8,128)(2,1)S(1)}, u32[]{:S(2)}, u32[]{:S(2)}) async-start(bf16[32,16,512]{2,1,0:T(8,128)(2,1)} %bitcast.64), calls=%async_computation.3 | async-start | bytes 1048576 | tf_op jit(solution)/shard_map/all_to_all | solution.py:27
  109.4 3.1 %shard_map.154 = (bf16[4,3,64,512]{3,2,1,0:T(8,128)(2,1)}, bf16[4,3,64,512]{3,2,1,0:T(8,128)(2,1)}) custom-call(s32[1]{0:T(128)} %bitcast.9.core, bf16[384,512]{1,0:T(8,128)(2,1)} %get-tuple-element.83.gathered, bf16[384,512]{1,0:T(8,128)(2,1)} %get-tuple-element.90.grad_pair, bf16[64,512]{1,0:T(8,128)(2,1)} %get-tuple-element.68.latent, ...), custom_call_target="tpu_custom_call" | custom-call | flops 268435456 | bytes 2621444 | tf_op jit(solution)/shard_map/pallas_call | solution.py:114
  115.9 3.3 %shard_map.155 = (bf16[384,512]{1,0:T(8,128)(2,1)}, bf16[384,512]{1,0:T(8,128)(2,1)}, bf16[384,512]{1,0:T(8,128)(2,1)}, bf16[384,512]{1,0:T(8,128)(2,1)}) custom-call(s32[1]{0:T(128)} %bitcast.16.chip, bf16[4,192,512]{2,1,0:T(8,128)(2,1)} %bitcast.59, bf16[4,192,512]{2,1,0:T(8,128)(2,1)} %bitcast.60, bf16[4,192,512]{2,1,0:T(8,128)(2,1)} %bitcast.61, ...), custom_call_target="tpu_custom_call" | custom-call | bytes 4718596 | tf_op jit(solution)/shard_map/pallas_call | solution.py:114
  119.1 5.2 %all-to-all-done.3 = bf16[32,16,512]{2,1,0:T(8,128)(2,1)S(1)} async-done(((bf16[32,16,512]{2,1,0:T(8,128)(2,1)}), bf16[32,16,512]{2,1,0:T(8,128)(2,1)S(1)}, u32[]{:S(2)}, u32[]{:S(2)}) %all-to-all-start.3) | async-done | bytes 524320 | tf_op jit(solution)/shard_map/all_to_all | solution.py:27
  125.1 2.7 %shard_map.156 = (bf16[64,512]{1,0:T(8,128)(2,1)}, bf16[64,512]{1,0:T(8,128)(2,1)}) custom-call(f32[64,512]{1,0:T(8,128)} %get-tuple-element.86.upstream, bf16[512,512]{1,0:T(8,128)(2,1)} %bitcast.55, s32[1,512]{1,0:T(1,128)} %reshape.88.sends, bf16[64,512]{1,0:T(8,128)(2,1)} %get-tuple-element.101.mesh_sum, bf16[2,512,512]{2,1,0:T(8,128)(2,1)} %w_edge.3, ...), custom_call_target="tpu_custom_call" | custom-call | flops 100663296 | bytes 1910784 | tf_op jit(solution)/shard_map/pallas_call | solution.py:114
  129.4 2.9 %collective-permute-start.9 = (bf16[384,512]{1,0:T(8,128)(2,1)}, bf16[384,512]{1,0:T(8,128)(2,1)S(1)}, u32[]{:S(2)}, u32[]{:S(2)}) collective-permute-start(bf16[384,512]{1,0:T(8,128)(2,1)} %get-tuple-element.116), channel_id=1, source_target_pairs={{0,128},{32,160},{64,192},{96,224},{128,0},{160,32},{192,64},{224,... | collective-permute-start | bytes 1179656 | tf_op jit(solution)/shard_map/ppermute | solution.py:37
  139.0 6.6 %shard_map.157 = (bf16[512,640]{1,0:T(8,128)(2,1)}, bf16[512,640]{1,0:T(8,128)(2,1)}) custom-call(s32[1,3]{1,0:T(1,128)} %counts.3, s32[1]{0:T(128)} %bitcast.9.core, f32[2,256]{1,0:T(2,128)} %copy-done.14, f32[2,256]{1,0:T(2,128)} %get-tuple-element.140.info_own, f32[2,256]{1,0:T(2,128)} %copy-done.13, bf16[64,512]{1,0:T(8,128)(2,1)} %copy-done.16, ...), custom_call_target="tpu_custom_call" | custom-call | flops 1610612736 | bytes 6344720 | tf_op jit(solution)/shard_map/pallas_call | solution.py:114
  149.0 3.3 %shard_map.158 = bf16[512,1024]{1,0:T(8,128)(2,1)} custom-call(bf16[512,640]{1,0:T(8,128)(2,1)} %get-tuple-element.118.kept, bf16[512,640]{1,0:T(8,128)(2,1)} %copy-done.5, bf16[384,512]{1,0:T(8,128)(2,1)} %get-tuple-element.120.refs_0_, bf16[384,512]{1,0:T(8,128)(2,1)} %copy-done.6, bf16[384,512]{1,0:T(8,128)(2,1)} %copy-done.7, bf16[384,512]{1,0:T(8,128)(2,1)} %copy-done.8), custom_call_target="tpu_custom_call" | custom-call | bytes 3932160 | tf_op jit(solution)/shard_map/pallas_call | solution.py:114
  152.2 38.4 %all_to_all.36.blocks = bf16[32,16,1024]{2,1,0:T(8,128)(2,1)} all-to-all(bf16[32,16,1024]{2,1,0:T(8,128)(2,1)} %bitcast.53), channel_id=1, replica_groups=mesh['grid'=8,'mesh'=32] {'mesh'}, dimensions={0} | all-to-all | bytes 2097152 | tf_op jit(solution)/shard_map/all_to_all | solution.py:27
  192.7 10.8 %all_to_all.37 = bf16[8,16,1024]{2,1,0:T(8,128)(2,1)S(1)} all-to-all(bf16[8,16,1024]{2,1,0:T(8,128)(2,1)} %shard_map.159), channel_id=1, replica_groups=mesh['grid'=8,'mesh'=32] {'grid'}, dimensions={0} | all-to-all | bytes 524288 | tf_op jit(solution)/shard_map/all_to_all | solution.py:27
  204.5 5.6 %all-to-all-start.6 = ((bf16[32,16,256]{2,1,0:T(8,128)(2,1)}), bf16[32,16,256]{2,1,0:T(8,128)(2,1)S(1)}, u32[]{:S(2)}, u32[]{:S(2)}) async-start(bf16[32,16,256]{2,1,0:T(8,128)(2,1)} %broadcast_in_dim.2), calls=%async_computation.6 | async-start | bytes 524288 | tf_op jit(solution)/shard_map/all_to_all | solution.py:27
  211.9 10.1 %all-to-all-done.6 = bf16[32,16,256]{2,1,0:T(8,128)(2,1)S(1)} async-done(((bf16[32,16,256]{2,1,0:T(8,128)(2,1)}), bf16[32,16,256]{2,1,0:T(8,128)(2,1)S(1)}, u32[]{:S(2)}, u32[]{:S(2)}) %all-to-all-start.6) | async-done | bytes 262176 | tf_op jit(solution)/shard_map/all_to_all | solution.py:27
  (81 shorter events, 38.6 us)
Async XLA Ops:
  0.6 19.7 %copy-start.11 = (s32[32,16]{0,1:T(8,128)S(1)}, s32[32,16]{0,1:T(8,128)}, u32[]{:S(2)}) copy-start(s32[32,16]{0,1:T(8,128)} %param.17) | copy-start | bytes 6148
  2.6 6.5 %collective-permute-start.1 = (f32[2,256]{1,0:T(2,128)S(1)}, f32[2,256]{1,0:T(2,128)S(1)}, u32[]{:S(2)}, u32[]{:S(2)}) collective-permute-start(f32[2,256]{1,0:T(2,128)S(1)} %get-tuple-element.138), channel_id=1, source_target_pairs={{1,0},{2,1},{3,2},{4,3},{5,4},{6,5},{7,6},{8,7},{9,8},{10,9},{11,1... | collective-permute-start | bytes 6152 | tf_op jit(solution)/shard_map/ppermute | solution.py:23
  4.5 7.9 %collective-permute-start = (f32[2,256]{1,0:T(2,128)S(1)}, f32[2,256]{1,0:T(2,128)S(1)}, u32[]{:S(2)}, u32[]{:S(2)}) collective-permute-start(f32[2,256]{1,0:T(2,128)S(1)} %get-tuple-element.139), channel_id=1, source_target_pairs={{0,1},{1,2},{2,3},{3,4},{4,5},{5,6},{6,7},{7,8},{8,9},{9,10},{10,1... | collective-permute-start | bytes 6152 | tf_op jit(solution)/shard_map/ppermute | solution.py:23
  4.7 33.4 %copy-start.12 = (s32[64,6]{0,1:T(8,128)S(1)}, s32[64,6]{0,1:T(8,128)}, u32[]{:S(2)}) copy-start(s32[64,6]{0,1:T(8,128)} %param.18) | copy-start | bytes 4612
  9.2 3.2 %copy-start.13 = (f32[2,256]{1,0:T(2,128)}, f32[2,256]{1,0:T(2,128)S(1)}, u32[]{:S(2)}) copy-start(f32[2,256]{1,0:T(2,128)S(1)} %collective-permute-done.1.info_east) | copy-start | bytes 6148
  15.0 7.8 %collective-permute-start.2 = (bf16[64,512]{1,0:T(8,128)(2,1)}, bf16[64,512]{1,0:T(8,128)(2,1)S(1)}, u32[]{:S(2)}, u32[]{:S(2)}) collective-permute-start(bf16[64,512]{1,0:T(8,128)(2,1)} %get-tuple-element.66), channel_id=1, source_target_pairs={{0,1},{1,2},{2,3},{3,4},{4,5},{5,6},{6,7},{7,8},{8,9},{9,10},{10,1... | collective-permute-start | bytes 196616 | tf_op jit(solution)/shard_map/ppermute | solution.py:23
  15.0 7.8 %collective-permute-start.3 = (bf16[64,512]{1,0:T(8,128)(2,1)}, bf16[64,512]{1,0:T(8,128)(2,1)S(1)}, u32[]{:S(2)}, u32[]{:S(2)}) collective-permute-start(bf16[64,512]{1,0:T(8,128)(2,1)} %get-tuple-element.67), channel_id=1, source_target_pairs={{1,0},{2,1},{3,2},{4,3},{5,4},{6,5},{7,6},{8,7},{9,8},{10,9},{11,1... | collective-permute-start | bytes 196616 | tf_op jit(solution)/shard_map/ppermute | solution.py:23
  26.0 27.1 %all-to-all-start = ((bf16[32,16,512]{2,1,0:T(8,128)(2,1)}), bf16[32,16,512]{2,1,0:T(8,128)(2,1)S(1)}, u32[]{:S(2)}, u32[]{:S(2)}) async-start(bf16[32,16,512]{2,1,0:T(8,128)(2,1)} %bitcast.66), calls=%async_computation | async-start | bytes 1048576 | tf_op jit(solution)/shard_map/all_to_all | solution.py:27
  81.6 18.4 %all-to-all-start.2 = ((bf16[32,16,512]{2,1,0:T(8,128)(2,1)}), bf16[32,16,512]{2,1,0:T(8,128)(2,1)S(1)}, u32[]{:S(2)}, u32[]{:S(2)}) async-start(bf16[32,16,512]{2,1,0:T(8,128)(2,1)} %bitcast.65), calls=%async_computation.2 | async-start | bytes 1048576 | tf_op jit(solution)/shard_map/all_to_all | solution.py:27
  89.1 2.5 %collective-permute-start.4 = (bf16[4,3,64,512]{3,2,1,0:T(8,128)(2,1)}, bf16[4,3,64,512]{3,2,1,0:T(8,128)(2,1)S(1)}, u32[]{:S(2)}, u32[]{:S(2)}) collective-permute-start(bf16[4,3,64,512]{3,2,1,0:T(8,128)(2,1)} %get-tuple-element.81), channel_id=1, source_target_pairs={{0,32},{32,0},{64,96},{96,64},{128,160},{160,128},{192,224},{224,1... | collective-permute-start | bytes 2359304 | tf_op jit(solution)/shard_map/ppermute | solution.py:41
  91.6 23.3 %copy-start.3 = (bf16[4,3,64,512]{3,2,1,0:T(8,128)(2,1)}, bf16[4,3,64,512]{3,2,1,0:T(8,128)(2,1)S(1)}, u32[]{:S(2)}) copy-start(bf16[4,3,64,512]{3,2,1,0:T(8,128)(2,1)S(1)} %collective-permute-done.4) | copy-start | bytes 2359300
  104.9 19.4 %all-to-all-start.3 = ((bf16[32,16,512]{2,1,0:T(8,128)(2,1)}), bf16[32,16,512]{2,1,0:T(8,128)(2,1)S(1)}, u32[]{:S(2)}, u32[]{:S(2)}) async-start(bf16[32,16,512]{2,1,0:T(8,128)(2,1)} %bitcast.64), calls=%async_computation.3 | async-start | bytes 1048576 | tf_op jit(solution)/shard_map/all_to_all | solution.py:27
  112.4 2.5 %collective-permute-start.5 = (bf16[4,3,64,512]{3,2,1,0:T(8,128)(2,1)}, bf16[4,3,64,512]{3,2,1,0:T(8,128)(2,1)S(1)}, u32[]{:S(2)}, u32[]{:S(2)}) collective-permute-start(bf16[4,3,64,512]{3,2,1,0:T(8,128)(2,1)} %get-tuple-element.95), channel_id=1, source_target_pairs={{0,32},{32,0},{64,96},{96,64},{128,160},{160,128},{192,224},{224,1... | collective-permute-start | bytes 2359304 | tf_op jit(solution)/shard_map/ppermute | solution.py:41
  114.9 0.9 copy-start.4
  127.8 17.9 %collective-permute-start.8 = (bf16[384,512]{1,0:T(8,128)(2,1)}, bf16[384,512]{1,0:T(8,128)(2,1)S(1)}, u32[]{:S(2)}, u32[]{:S(2)}) collective-permute-start(bf16[384,512]{1,0:T(8,128)(2,1)} %get-tuple-element.115), channel_id=1, source_target_pairs={{0,64},{32,96},{64,128},{96,160},{128,192},{160,224},{192,0},{224,... | collective-permute-start | bytes 1179656 | tf_op jit(solution)/shard_map/ppermute | solution.py:37
  129.4 16.3 %collective-permute-start.9 = (bf16[384,512]{1,0:T(8,128)(2,1)}, bf16[384,512]{1,0:T(8,128)(2,1)S(1)}, u32[]{:S(2)}, u32[]{:S(2)}) collective-permute-start(bf16[384,512]{1,0:T(8,128)(2,1)} %get-tuple-element.116), channel_id=1, source_target_pairs={{0,128},{32,160},{64,192},{96,224},{128,0},{160,32},{192,64},{224,... | collective-permute-start | bytes 1179656 | tf_op jit(solution)/shard_map/ppermute | solution.py:37
  132.3 13.4 %collective-permute-start.10 = (bf16[384,512]{1,0:T(8,128)(2,1)}, bf16[384,512]{1,0:T(8,128)(2,1)S(1)}, u32[]{:S(2)}, u32[]{:S(2)}) collective-permute-start(bf16[384,512]{1,0:T(8,128)(2,1)} %get-tuple-element.117), channel_id=1, source_target_pairs={{0,192},{32,224},{64,0},{96,32},{128,64},{160,96},{192,128},{224,1... | collective-permute-start | bytes 1179656 | tf_op jit(solution)/shard_map/ppermute | solution.py:37
  133.6 4.5 %collective-permute-start.7 = (bf16[64,512]{1,0:T(8,128)(2,1)}, bf16[64,512]{1,0:T(8,128)(2,1)S(1)}, u32[]{:S(2)}, u32[]{:S(2)}) collective-permute-start(bf16[64,512]{1,0:T(8,128)(2,1)} %get-tuple-element.107.grad_own), channel_id=1, source_target_pairs={{1,0},{2,1},{3,2},{4,3},{5,4},{6,5},{7,6},{8,7},{9,8},{10,9},{11,1... | collective-permute-start | bytes 196616 | tf_op jit(solution)/shard_map/ppermute | solution.py:23
  133.6 4.8 %collective-permute-start.6 = (bf16[64,512]{1,0:T(8,128)(2,1)}, bf16[64,512]{1,0:T(8,128)(2,1)S(1)}, u32[]{:S(2)}, u32[]{:S(2)}) collective-permute-start(bf16[64,512]{1,0:T(8,128)(2,1)} %get-tuple-element.107.grad_own), channel_id=1, source_target_pairs={{0,1},{1,2},{2,3},{3,4},{4,5},{5,6},{6,7},{7,8},{8,9},{9,10},{10,1... | collective-permute-start | bytes 196616 | tf_op jit(solution)/shard_map/ppermute | solution.py:23
  145.7 2.4 %copy-start.6 = (bf16[384,512]{1,0:T(8,128)(2,1)}, bf16[384,512]{1,0:T(8,128)(2,1)S(1)}, u32[]{:S(2)}) copy-start(bf16[384,512]{1,0:T(8,128)(2,1)S(1)} %collective-permute-done.8.refs_1_) | copy-start | bytes 1179652
  145.7 2.4 %copy-start.7 = (bf16[384,512]{1,0:T(8,128)(2,1)}, bf16[384,512]{1,0:T(8,128)(2,1)S(1)}, u32[]{:S(2)}) copy-start(bf16[384,512]{1,0:T(8,128)(2,1)S(1)} %collective-permute-done.9.refs_2_) | copy-start | bytes 1179652
  145.7 2.4 %copy-start.8 = (bf16[384,512]{1,0:T(8,128)(2,1)}, bf16[384,512]{1,0:T(8,128)(2,1)S(1)}, u32[]{:S(2)}) copy-start(bf16[384,512]{1,0:T(8,128)(2,1)S(1)} %collective-permute-done.10.refs_3_) | copy-start | bytes 1179652
  145.7 2.4 %collective-permute-start.11 = (bf16[512,640]{1,0:T(8,128)(2,1)}, bf16[512,640]{1,0:T(8,128)(2,1)S(1)}, u32[]{:S(2)}, u32[]{:S(2)}) collective-permute-start(bf16[512,640]{1,0:T(8,128)(2,1)} %get-tuple-element.119), channel_id=1, source_target_pairs={{0,32},{32,0},{64,96},{96,64},{128,160},{160,128},{192,224},{224,1... | collective-permute-start | bytes 1966088 | tf_op jit(solution)/shard_map/ppermute | solution.py:41
  204.5 17.6 %all-to-all-start.6 = ((bf16[32,16,256]{2,1,0:T(8,128)(2,1)}), bf16[32,16,256]{2,1,0:T(8,128)(2,1)S(1)}, u32[]{:S(2)}, u32[]{:S(2)}) async-start(bf16[32,16,256]{2,1,0:T(8,128)(2,1)} %broadcast_in_dim.2), calls=%async_computation.6 | async-start | bytes 524288 | tf_op jit(solution)/shard_map/all_to_all | solution.py:27
  (9 other events, 6.4 us)
where the time goes:
time: 224 us; the launch traced here: 223 us
  blocking collectives  68.3 us (30%)
  waiting for transfers between devices  53 us (24%)
  Pallas kernels  46 us (21%)
  starting transfers between devices  41.9 us (19%)
  local copies, waits for them, and re-layouts  11 us (5%)
    all_to_all x3, blocking collectives, exchange(): return lax.all_to_all(blocks, axis, split_axis=0, concat_axis=0, tiled=True)  68.3 us
    pallas_call x13, Pallas kernels, call(): pl.pallas_call(kernel, grid=(1,), in_specs=specs, out_specs=[pl.BlockSpec...  46 us
    all_to_all x4, waiting for transfers between devices, exchange(): return lax.all_to_all(blocks, axis, split_axis=0, concat_axis=0, tiled=True)  38 us
    all_to_all x4, starting transfers between devices, exchange(): return lax.all_to_all(blocks, axis, split_axis=0, concat_axis=0, tiled=True)  26.6 us
    ppermute x3, waiting for transfers between devices, to_other_core(): lax.ppermute(block, 'grid', [(i, i ^ 1) for i in range(lax.axis_size('gri...  7.28 us
    ppermute x3, starting transfers between devices, from_sides(): lax.ppermute(to_west, 'mesh', backward)  7.2 us
    unnamed x36, local copies, waits for them, and re-layouts  7.07 us
    ppermute x3, starting transfers between devices, along_y(): lax.ppermute(block, 'grid', [(i, (i + 2 * step) % count) for i in range(c...  5.82 us
  transfers between devices with their start and end apart: 16, of which 11 were waited for; matrix products, arithmetic and copies ran while one was open for 1% of the time, Pallas kernels for 9%

commit v1 on v0

--- a/solution.py
+++ b/solution.py
@@ -59,8 +59,12 @@
 
 
 def silu_slope(values):
+    return silu_both(values)[1]
+
+
+def silu_both(values):
     logistic = jax.nn.sigmoid(values)
-    return logistic * (1.0 + values * (1.0 - logistic))
+    return values * logistic, logistic * (1.0 + values * (1.0 - logistic))
 
 
 def matmul(matrix_a, matrix_b):
@@ -119,12 +123,12 @@
             pl.BlockSpec(s.shape, lambda i, zeros=(0,) * len(s.shape): zeros) for s in shapes
         ],
         out_shape=shapes,
-        compiler_params=pltpu.CompilerParams(vmem_limit_bytes=60 * 2**20),
+        compiler_params=pltpu.CompilerParams(vmem_limit_bytes=64 * 2**20),
         cost_estimate=pl.CostEstimate(flops=flops, bytes_accessed=moved, transcendentals=0),
     )(*args)
 
 
-def edge_forward(counts, feats, sources, w_embed, w_edge, gains, pre_out, rows_out, edge_out, message_out):
+def edge_forward(counts, feats, sources, w_embed, w_edge, gains, pre_out, rows_out, slope_out, message_out):
     grid_pre = left_transposed(feats[...], w_embed[...])
     pre_out[...] = grid_pre
     normed, _ = normalize(silu(grid_pre))
@@ -133,11 +137,11 @@
     for side in range(3):
         chosen = live_hits(sources[side : side + 1], counts[0, side], latent.shape[0])
         rows = left_transposed(chosen, latent).astype(BF16)
-        edge_pre = matmul(rows, w_edge[...])
+        message, slope = silu_both(matmul(rows, w_edge[...]))
         place = pl.ds(side * slots, slots)
         rows_out[place] = rows
-        edge_out[place] = edge_pre
-        message_out[place] = silu(edge_pre).astype(BF16)
+        slope_out[place] = slope.astype(BF16)
+        message_out[place] = message.astype(BF16)
 
 
 def edge_sums(info_west, info_own, info_east, messages, west_out, own_out, east_out):
@@ -164,17 +168,17 @@
     far = left_transposed(hits(links - nodes, halo.shape[0]), halo)
     gathered = (own + far).astype(BF16)
     pair_pre = matmul(gathered, weights[0]).reshape(degree, nodes, width) + matmul(latent, weights[1])[None]
-    message = silu(pair_pre).astype(BF16)
-    node_sum = jnp.sum(message.astype(F32), axis=0).astype(BF16)
-    return gathered, pair_pre, node_sum, matmul(node_sum, weights[2])
-
-
-def layer_back(upstream, gain, gathered, pair_pre, node_out, links, weights, halo_rows):
-    degree, nodes, width = pair_pre.shape
+    message, slope = silu_both(pair_pre)
+    node_sum = jnp.sum(message.astype(BF16).astype(F32), axis=0).astype(BF16)
+    return gathered, slope, node_sum, matmul(node_sum, weights[2])
+
+
+def layer_back(upstream, gain, gathered, slope, node_out, links, weights, halo_rows):
+    degree, nodes, width = slope.shape
     normed, inverse = normalize(node_out)
     grad_norm = normalize_back(upstream * gain, normed, inverse).astype(BF16)
     grad_node = right_transposed(grad_norm, weights[2])
-    grad_pair_pre = grad_node[None] * silu_slope(pair_pre)
+    grad_pair_pre = grad_node[None] * slope
     grad_pair = grad_pair_pre.astype(BF16).reshape(degree * nodes, width)
     grad_self = jnp.sum(grad_pair_pre, axis=0).astype(BF16)
     grad_rows = right_transposed(grad_pair, weights[0]).astype(BF16)
@@ -184,18 +188,18 @@
 
 
 def layer_forward(
-    latent, halo, links, weights, gains, sends, gathered_out, pair_out, sum_out, node_out, latent_out, sent_out
+    latent, halo, links, weights, gains, sends, gathered_out, slope_out, sum_out, node_out, latent_out, sent_out
 ):
     nodes = latent.shape[0]
-    gathered, pair_pre, node_sum, node_pre = layer_values(
-        latent[...], halo[...], links[...], weights, pair_out.shape[0]
+    gathered, slope, node_sum, node_pre = layer_values(
+        latent[...], halo[...], links[...], weights, slope_out.shape[0]
     )
     normed, _ = normalize(node_pre)
     after = (latent[...].astype(F32) + normed * gains[2:3]).astype(BF16)
     latent_out[...] = after
     sent_out[...] = left_transposed(hits(sends[...], nodes), after).astype(BF16)
     gathered_out[...] = gathered
-    pair_out[...] = pair_pre
+    slope_out[...] = slope.astype(BF16)
     sum_out[...] = node_sum
     node_out[...] = node_pre
 
@@ -218,7 +222,7 @@
     up_out,
 ):
     nodes = latent.shape[0]
-    gathered, pair_pre, node_sum, node_pre = layer_values(
+    gathered, slope, node_sum, node_pre = layer_values(
         latent[...], halo[...], links[...], weights, links.shape[1] // nodes
     )
     normed, _ = normalize(node_pre)
@@ -227,7 +231,7 @@
     sum_out[...] = node_sum
     upstream = cotangent[...].astype(F32) * scale
     norm_out[...], pair_out[...], self_out[...], halo_out[...], up_out[...] = layer_back(
-        upstream, gains[3:4], gathered, pair_pre, node_pre, links[...], weights, halo.shape[0]
+        upstream, gains[3:4], gathered, slope, node_pre, links[...], weights, halo.shape[0]
     )
 
 
@@ -236,7 +240,7 @@
     returned,
     sends,
     gathered,
-    pair_pre,
+    slope,
     node_pre,
     links,
     weights,
@@ -250,7 +254,7 @@
     nodes = upstream.shape[0]
     total = upstream[...] + matmul(hits(sends[...], nodes), returned[...])
     norm_out[...], pair_out[...], self_out[...], halo_out[...], up_out[...] = layer_back(
-        total, gains[2:3], gathered[...], pair_pre[...], node_pre[...], links[...], weights, returned.shape[0]
+        total, gains[2:3], gathered[...], slope[...].astype(F32), node_pre[...], links[...], weights, returned.shape[0]
     )
 
 
@@ -292,7 +296,7 @@
     grad_west,
     grad_own,
     grad_east,
-    edge_pre,
+    edge_slope,
     edge_rows,
     grid_pre,
     feats,
@@ -315,7 +319,7 @@
     for side, (info, grads) in enumerate(sides):
         place = pl.ds(side * slots, slots)
         grad_message = left_transposed(weighted_hits(info[...], nodes), grads[...]).astype(BF16)
-        grad_edge = (grad_message.astype(F32) * silu_slope(edge_pre[place])).astype(BF16)
+        grad_edge = (grad_message.astype(F32) * edge_slope[place].astype(F32)).astype(BF16)
         edge_w += left_transposed(grad_edge, edge_rows[place])
         grad_rows = right_transposed(grad_edge, w_edge[...]).astype(BF16)
         chosen = live_hits(sources[side : side + 1], counts[0, side], grid_nodes)
@@ -392,12 +396,12 @@
     edge_info = jnp.stack([g2m_dst.astype(F32), g2m_weight.astype(F32)], axis=1)
     info_west, info_east = from_sides(edge_info[2], edge_info[0])
     info = [info_west, edge_info[1], info_east]
-    grid_pre, edge_rows, edge_pre, messages = call(
+    grid_pre, edge_rows, edge_slope, messages = call(
         edge_forward,
         [
             ((grid_nodes, width), F32),
             ((3 * slots, width), BF16),
-            ((3 * slots, width), F32),
+            ((3 * slots, width), BF16),
             ((3 * slots, width), BF16),
         ],
         [g2m_count, feats, g2m_src, w_embed, w_encode, gains],
@@ -420,11 +424,11 @@
         picked={3: 1},
     )
     halo = exchange(sent.reshape(peers, -1, width), "mesh").reshape(-1, width)
-    gathered, pair_pre, node_sum, node_pre, middle, sent = call(
+    gathered, pair_slope, node_sum, node_pre, middle, sent = call(
         layer_forward,
         [
             ((pairs, width), BF16),
-            ((degree, nodes, width), F32),
+            ((degree, nodes, width), BF16),
             ((nodes, width), BF16),
             ((nodes, width), F32),
             ((nodes, width), BF16),
@@ -469,7 +473,7 @@
     grad_norm, grad_pair, grad_self, grad_halo, upstream = call(
         layer_first_back,
         back_shapes,
-        [upstream, returned, sends, gathered, pair_pre, node_pre, links, w_layers, gains],
+        [upstream, returned, sends, gathered, pair_slope, node_pre, links, w_layers, gains],
         unit * pairs * 3,
         picked={7: 0},
     )
@@ -502,7 +506,7 @@
             grad_west,
             grad_sum,
             grad_east,
-            edge_pre,
+            edge_slope,
             edge_rows,
             grid_pre,
             feats,

time: 224 us -> 220 us (0.982)
  local copies, waits for them, and re-layouts: 11 us -> 6.41 us
    unnamed x36 -> x2, local copies, waits for them, and re-layouts: 7.07 us -> 1.74 us
  transfers between devices with their start and end apart: 16 -> 16, of which waited for: 11 -> 12; matrix products, arithmetic and copies ran while one was open for 1% -> 2% of each run, Pallas kernels for 9% -> 9%
where the time goes in v1:
time: 220 us; the launch traced here: 219 us
  blocking collectives  67.7 us (31%)
  waiting for transfers between devices  54 us (25%)
  Pallas kernels  45.8 us (21%)
  starting transfers between devices  42.4 us (19%)
  local copies, waits for them, and re-layouts  6.41 us (3%)
    all_to_all x3, blocking collectives, exchange(): return lax.all_to_all(blocks, axis, split_axis=0, concat_axis=0, tiled=True)  67.7 us
    pallas_call x13, Pallas kernels, call(): pl.pallas_call(kernel, grid=(1,), in_specs=specs, out_specs=[pl.BlockSpec...  45.8 us
    all_to_all x4, waiting for transfers between devices, exchange(): return lax.all_to_all(blocks, axis, split_axis=0, concat_axis=0, tiled=True)  38.2 us
    all_to_all x4, starting transfers between devices, exchange(): return lax.all_to_all(blocks, axis, split_axis=0, concat_axis=0, tiled=True)  27.2 us
    ppermute x3, waiting for transfers between devices, to_other_core(): lax.ppermute(block, 'grid', [(i, i ^ 1) for i in range(lax.axis_size('gri...  7.69 us
    ppermute x3, starting transfers between devices, from_sides(): lax.ppermute(to_west, 'mesh', backward)  7.19 us
    ppermute x3, starting transfers between devices, along_y(): lax.ppermute(block, 'grid', [(i, (i + 2 * step) % count) for i in range(c...  5.83 us
    ppermute x3, waiting for transfers between devices, from_sides(): lax.ppermute(to_east, 'mesh', forward)  4.9 us
  transfers between devices with their start and end apart: 16, of which 12 were waited for; matrix products, arithmetic and copies ran while one was open for 2% of the time, Pallas kernels for 9%

profile of v1, /device:TPU:32, one launch (start us, length us, event | category | flops | bytes accessed | tf_op | source)
XLA Modules:
  0.0 219.1 jit_solution(12318231619494563104)
XLA Ops:
  4.7 4.5 %shard_map.147 = (f32[512,512]{1,0:T(8,128)}, bf16[768,512]{1,0:T(8,128)(2,1)}, bf16[768,512]{1,0:T(8,128)(2,1)}, bf16[768,512]{1,0:T(8,128)(2,1)}) custom-call(s32[1,3]{1,0:T(1,128)} %counts.3, bf16[227,512]{1,0:T(8,128)(2,1)} %bitcast.65, s32[3,256]{1,0:T(4,128)} %sources.3, bf16[227,512]{1,0:T(8,128)(2,1)} %w_embed.1, bf16[2,512,512]{2,1,0:T(8,128)(2,1)} %w_edge.3, ...), custom_call_target="tpu_custom_call" | custom-call | flops 1073741824 | bytes 4932620 | tf_op jit(solution)/shard_map/pallas_call | solution.py:118
  9.2 3.5 %collective-permute-done.info_west = f32[2,256]{1,0:T(2,128)} collective-permute-done((f32[2,256]{1,0:T(2,128)}, f32[2,256]{1,0:T(2,128)}, u32[]{:S(2)}, u32[]{:S(2)}) %collective-permute-start) | collective-permute-done | bytes 2080 | tf_op jit(solution)/shard_map/ppermute | solution.py:23
  14.7 5.3 %collective-permute-start.3 = (bf16[64,512]{1,0:T(8,128)(2,1)}, bf16[64,512]{1,0:T(8,128)(2,1)}, u32[]{:S(2)}, u32[]{:S(2)}) collective-permute-start(bf16[64,512]{1,0:T(8,128)(2,1)} %get-tuple-element.67), channel_id=1, source_target_pairs={{1,0},{2,1},{3,2},{4,3},{5,4},{6,5},{7,6},{8,7},{9,8},{10,9},{11,1... | collective-permute-start | bytes 196616 | tf_op jit(solution)/shard_map/ppermute | solution.py:23
  25.2 12.2 %all-to-all-start = ((bf16[32,16,512]{2,1,0:T(8,128)(2,1)}), bf16[32,16,512]{2,1,0:T(8,128)(2,1)}, u32[]{:S(2)}, u32[]{:S(2)}) async-start(bf16[32,16,512]{2,1,0:T(8,128)(2,1)} %bitcast.61), calls=%async_computation | async-start | bytes 1048576 | tf_op jit(solution)/shard_map/all_to_all | solution.py:27
  38.7 13.7 %all-to-all-done = bf16[32,16,512]{2,1,0:T(8,128)(2,1)} async-done(((bf16[32,16,512]{2,1,0:T(8,128)(2,1)}), bf16[32,16,512]{2,1,0:T(8,128)(2,1)}, u32[]{:S(2)}, u32[]{:S(2)}) %all-to-all-start) | async-done | bytes 524320 | tf_op jit(solution)/shard_map/all_to_all | solution.py:27
  52.4 4.1 %shard_map.150 = (bf16[384,512]{1,0:T(8,128)(2,1)}, bf16[6,64,512]{2,1,0:T(8,128)(2,1)}, bf16[64,512]{1,0:T(8,128)(2,1)}, f32[64,512]{1,0:T(8,128)}, bf16[64,512]{1,0:T(8,128)(2,1)}, /*index=5*/bf16[512,512]{1,0:T(8,128)(2,1)}) custom-call(bf16[64,512]{1,0:T(8,128)(2,1)} %get-tuple-element.68.latent, bf16[512,512]{1,0:T(8,128)(2,1)} %bitcast.5.halo, ...), custom_call_target="tpu_custom_call" | custom-call | flops 402653184 | bytes 5320192 | tf_op jit(solution)/shard_map/pallas_call | solution.py:118
  56.4 19.1 %all_to_all.35 = bf16[32,16,512]{2,1,0:T(8,128)(2,1)} all-to-all(bf16[32,16,512]{2,1,0:T(8,128)(2,1)} %bitcast.62), channel_id=1, replica_groups=mesh['grid'=8,'mesh'=32] {'mesh'}, dimensions={0} | all-to-all | bytes 1048576 | tf_op jit(solution)/shard_map/all_to_all | solution.py:27
  75.5 4.7 %shard_map.151 = (bf16[64,512]{1,0:T(8,128)(2,1)}, bf16[384,512]{1,0:T(8,128)(2,1)}, bf16[64,512]{1,0:T(8,128)(2,1)}, bf16[64,512]{1,0:T(8,128)(2,1)}, bf16[384,...) custom-call(f32[1]{0:T(128)} %constant.26.clone.1.scale, ...), custom_call_target="tpu_custom_call" | custom-call | flops 805306368 | bytes 5514756 | tf_op jit(solution)/shard_map/pallas_call | solution.py:118
  80.2 4.8 %all-to-all-start.2 = ((bf16[32,16,512]{2,1,0:T(8,128)(2,1)}), bf16[32,16,512]{2,1,0:T(8,128)(2,1)}, u32[]{:S(2)}, u32[]{:S(2)}) async-start(bf16[32,16,512]{2,1,0:T(8,128)(2,1)} %bitcast.60), calls=%async_computation.2 | async-start | bytes 1048576 | tf_op jit(solution)/shard_map/all_to_all | solution.py:27
  85.0 3.1 %shard_map.152 = (bf16[4,3,64,512]{3,2,1,0:T(8,128)(2,1)}, bf16[4,3,64,512]{3,2,1,0:T(8,128)(2,1)}) custom-call(s32[1]{0:T(128)} %bitcast.9.core, bf16[384,512]{1,0:T(8,128)(2,1)} %get-tuple-element.75.gathered, bf16[384,512]{1,0:T(8,128)(2,1)} %get-tuple-element.76.grad_pair, bf16[64,512]{1,0:T(8,128)(2,1)} %get-tuple-element.70.refs_0_.latent, ...), custom_call_target="tpu_custom_call" | custom-call | flops 268435456 | bytes 2621444 | tf_op jit(solution)/shard_map/pallas_call | solution.py:118
  90.7 8.2 %all-to-all-done.2 = bf16[32,16,512]{2,1,0:T(8,128)(2,1)} async-done(((bf16[32,16,512]{2,1,0:T(8,128)(2,1)}), bf16[32,16,512]{2,1,0:T(8,128)(2,1)}, u32[]{:S(2)}, u32[]{:S(2)}) %all-to-all-start.2) | async-done | bytes 524320 | tf_op jit(solution)/shard_map/all_to_all | solution.py:27
  98.9 4.0 %shard_map.153 = (bf16[64,512]{1,0:T(8,128)(2,1)}, bf16[384,512]{1,0:T(8,128)(2,1)}, bf16[64,512]{1,0:T(8,128)(2,1)}, bf16[512,512]{1,0:T(8,128)(2,1)}, f32[64,512]{1,0:T(8,128)}) custom-call(f32[64,512]{1,0:T(8,128)} %get-tuple-element.73.upstream, bf16[512,512]{1,0:T(8,128)(2,1)} %bitcast.11.returned, s32[1,512]{1,0:T(1,128)} %reshape.88.sends, ...), custom_call_target="tpu_custom_call" | custom-call | flops 603979776 | bytes 5910016 | tf_op jit(solution)/shard_map/pallas_call | solution.py:118
  102.9 4.6 %all-to-all-start.3 = ((bf16[32,16,512]{2,1,0:T(8,128)(2,1)}), bf16[32,16,512]{2,1,0:T(8,128)(2,1)}, u32[]{:S(2)}, u32[]{:S(2)}) async-start(bf16[32,16,512]{2,1,0:T(8,128)(2,1)} %bitcast.59), calls=%async_computation.3 | async-start | bytes 1048576 | tf_op jit(solution)/shard_map/all_to_all | solution.py:27
  107.5 3.1 %shard_map.154 = (bf16[4,3,64,512]{3,2,1,0:T(8,128)(2,1)}, bf16[4,3,64,512]{3,2,1,0:T(8,128)(2,1)}) custom-call(s32[1]{0:T(128)} %bitcast.9.core, bf16[384,512]{1,0:T(8,128)(2,1)} %get-tuple-element.83.gathered, bf16[384,512]{1,0:T(8,128)(2,1)} %get-tuple-element.90.grad_pair, bf16[64,512]{1,0:T(8,128)(2,1)} %get-tuple-element.68.latent, ...), custom_call_target="tpu_custom_call" | custom-call | flops 268435456 | bytes 2621444 | tf_op jit(solution)/shard_map/pallas_call | solution.py:118
  113.2 3.3 %shard_map.155 = (bf16[384,512]{1,0:T(8,128)(2,1)}, bf16[384,512]{1,0:T(8,128)(2,1)}, bf16[384,512]{1,0:T(8,128)(2,1)}, bf16[384,512]{1,0:T(8,128)(2,1)}) custom-call(s32[1]{0:T(128)} %bitcast.16.chip, bf16[4,192,512]{2,1,0:T(8,128)(2,1)} %bitcast.56, bf16[4,192,512]{2,1,0:T(8,128)(2,1)} %bitcast.13.last_other, bf16[4,192,512]{2,1,0:T(8,128)(2,1)} %bitcast.57, ...), custom_call_target="tpu_custom_call" | custom-call | bytes 4718596 | tf_op jit(solution)/shard_map/pallas_call | solution.py:118
  116.5 6.1 %all-to-all-done.3 = bf16[32,16,512]{2,1,0:T(8,128)(2,1)} async-done(((bf16[32,16,512]{2,1,0:T(8,128)(2,1)}), bf16[32,16,512]{2,1,0:T(8,128)(2,1)}, u32[]{:S(2)}, u32[]{:S(2)}) %all-to-all-start.3) | async-done | bytes 524320 | tf_op jit(solution)/shard_map/all_to_all | solution.py:27
  122.7 2.7 %shard_map.156 = (bf16[64,512]{1,0:T(8,128)(2,1)}, bf16[64,512]{1,0:T(8,128)(2,1)}) custom-call(f32[64,512]{1,0:T(8,128)} %get-tuple-element.86.upstream, bf16[512,512]{1,0:T(8,128)(2,1)} %bitcast.15.returned, s32[1,512]{1,0:T(1,128)} %reshape.88.sends, bf16[64,512]{1,0:T(8,128)(2,1)} %get-tuple-element.101.mesh_sum, bf16[2,512,512]{2,1,0:T(8,128)(2,1)} %w_edge.3, ...), custom_call_target="tpu_custom_call" | custom-call | flops 100663296 | bytes 1910784 | tf_op jit(solution)/shard_map/pallas_call | solution.py:118
  126.9 2.9 %collective-permute-start.9 = (bf16[384,512]{1,0:T(8,128)(2,1)}, bf16[384,512]{1,0:T(8,128)(2,1)}, u32[]{:S(2)}, u32[]{:S(2)}) collective-permute-start(bf16[384,512]{1,0:T(8,128)(2,1)} %get-tuple-element.116), channel_id=1, source_target_pairs={{0,128},{32,160},{64,192},{96,224},{128,0},{160,32},{192,64},{224,... | collective-permute-start | bytes 1179656 | tf_op jit(solution)/shard_map/ppermute | solution.py:37
  136.1 6.4 %shard_map.157 = (bf16[512,640]{1,0:T(8,128)(2,1)}, bf16[512,640]{1,0:T(8,128)(2,1)}) custom-call(s32[1,3]{1,0:T(1,128)} %counts.3, s32[1]{0:T(128)} %bitcast.9.core, f32[2,256]{1,0:T(2,128)} %collective-permute-done.info_west, f32[2,256]{1,0:T(2,128)} %get-tuple-element.140.info_own, f32[2,256]{1,0:T(2,128)} %collective-permute-done.1.info_east, ...), custom_call_target="tpu_custom_call" | custom-call | flops 1610612736 | bytes 5558288 | tf_op jit(solution)/shard_map/pallas_call | solution.py:118
  145.6 3.3 %shard_map.158 = bf16[512,1024]{1,0:T(8,128)(2,1)} custom-call(bf16[512,640]{1,0:T(8,128)(2,1)} %get-tuple-element.118.kept, bf16[512,640]{1,0:T(8,128)(2,1)} %collective-permute-done.11.other, bf16[384,512]{1,0:T(8,128)(2,1)} %get-tuple-element.120.refs_0_, bf16[384,512]{1,0:T(8,128)(2,1)} %collective-permute-done.8.refs_1_, ...), custom_call_target="tpu_custom_call" | custom-call | bytes 3932160 | tf_op jit(solution)/shard_map/pallas_call | solution.py:118
  148.9 37.7 %all_to_all.36.blocks = bf16[32,16,1024]{2,1,0:T(8,128)(2,1)} all-to-all(bf16[32,16,1024]{2,1,0:T(8,128)(2,1)} %bitcast.53), channel_id=1, replica_groups=mesh['grid'=8,'mesh'=32] {'mesh'}, dimensions={0} | all-to-all | bytes 2097152 | tf_op jit(solution)/shard_map/all_to_all | solution.py:27
  188.7 10.8 %all_to_all.37 = bf16[8,16,1024]{2,1,0:T(8,128)(2,1)S(1)} all-to-all(bf16[8,16,1024]{2,1,0:T(8,128)(2,1)} %shard_map.159), channel_id=1, replica_groups=mesh['grid'=8,'mesh'=32] {'grid'}, dimensions={0} | all-to-all | bytes 524288 | tf_op jit(solution)/shard_map/all_to_all | solution.py:27
  200.6 5.6 %all-to-all-start.6 = ((bf16[32,16,256]{2,1,0:T(8,128)(2,1)}), bf16[32,16,256]{2,1,0:T(8,128)(2,1)S(1)}, u32[]{:S(2)}, u32[]{:S(2)}) async-start(bf16[32,16,256]{2,1,0:T(8,128)(2,1)} %broadcast_in_dim.2), calls=%async_computation.6 | async-start | bytes 524288 | tf_op jit(solution)/shard_map/all_to_all | solution.py:27
  208.0 10.1 %all-to-all-done.6 = bf16[32,16,256]{2,1,0:T(8,128)(2,1)S(1)} async-done(((bf16[32,16,256]{2,1,0:T(8,128)(2,1)}), bf16[32,16,256]{2,1,0:T(8,128)(2,1)S(1)}, u32[]{:S(2)}, u32[]{:S(2)}) %all-to-all-start.6) | async-done | bytes 262176 | tf_op jit(solution)/shard_map/all_to_all | solution.py:27
  (47 shorter events, 34.6 us)
Async XLA Ops:
  2.6 6.6 %collective-permute-start.1 = (f32[2,256]{1,0:T(2,128)}, f32[2,256]{1,0:T(2,128)}, u32[]{:S(2)}, u32[]{:S(2)}) collective-permute-start(f32[2,256]{1,0:T(2,128)} %get-tuple-element.138), channel_id=1, source_target_pairs={{1,0},{2,1},{3,2},{4,3},{5,4},{6,5},{7,6},{8,7},{9,8},{10,9},{11,1... | collective-permute-start | bytes 6152 | tf_op jit(solution)/shard_map/ppermute | solution.py:23
  4.5 8.2 %collective-permute-start = (f32[2,256]{1,0:T(2,128)}, f32[2,256]{1,0:T(2,128)}, u32[]{:S(2)}, u32[]{:S(2)}) collective-permute-start(f32[2,256]{1,0:T(2,128)} %get-tuple-element.139), channel_id=1, source_target_pairs={{0,1},{1,2},{2,3},{3,4},{4,5},{5,6},{6,7},{7,8},{8,9},{9,10},{10,1... | collective-permute-start | bytes 6152 | tf_op jit(solution)/shard_map/ppermute | solution.py:23
  14.7 7.9 %collective-permute-start.2 = (bf16[64,512]{1,0:T(8,128)(2,1)}, bf16[64,512]{1,0:T(8,128)(2,1)}, u32[]{:S(2)}, u32[]{:S(2)}) collective-permute-start(bf16[64,512]{1,0:T(8,128)(2,1)} %get-tuple-element.66), channel_id=1, source_target_pairs={{0,1},{1,2},{2,3},{3,4},{4,5},{5,6},{6,7},{7,8},{8,9},{9,10},{10,1... | collective-permute-start | bytes 196616 | tf_op jit(solution)/shard_map/ppermute | solution.py:23
  14.7 7.9 %collective-permute-start.3 = (bf16[64,512]{1,0:T(8,128)(2,1)}, bf16[64,512]{1,0:T(8,128)(2,1)}, u32[]{:S(2)}, u32[]{:S(2)}) collective-permute-start(bf16[64,512]{1,0:T(8,128)(2,1)} %get-tuple-element.67), channel_id=1, source_target_pairs={{1,0},{2,1},{3,2},{4,3},{5,4},{6,5},{7,6},{8,7},{9,8},{10,9},{11,1... | collective-permute-start | bytes 196616 | tf_op jit(solution)/shard_map/ppermute | solution.py:23
  25.2 27.2 %all-to-all-start = ((bf16[32,16,512]{2,1,0:T(8,128)(2,1)}), bf16[32,16,512]{2,1,0:T(8,128)(2,1)}, u32[]{:S(2)}, u32[]{:S(2)}) async-start(bf16[32,16,512]{2,1,0:T(8,128)(2,1)} %bitcast.61), calls=%async_computation | async-start | bytes 1048576 | tf_op jit(solution)/shard_map/all_to_all | solution.py:27
  80.2 18.7 %all-to-all-start.2 = ((bf16[32,16,512]{2,1,0:T(8,128)(2,1)}), bf16[32,16,512]{2,1,0:T(8,128)(2,1)}, u32[]{:S(2)}, u32[]{:S(2)}) async-start(bf16[32,16,512]{2,1,0:T(8,128)(2,1)} %bitcast.60), calls=%async_computation.2 | async-start | bytes 1048576 | tf_op jit(solution)/shard_map/all_to_all | solution.py:27
  88.1 2.6 %collective-permute-start.4 = (bf16[4,3,64,512]{3,2,1,0:T(8,128)(2,1)}, bf16[4,3,64,512]{3,2,1,0:T(8,128)(2,1)}, u32[]{:S(2)}, u32[]{:S(2)}) collective-permute-start(bf16[4,3,64,512]{3,2,1,0:T(8,128)(2,1)} %get-tuple-element.81), channel_id=1, source_target_pairs={{0,32},{32,0},{64,96},{96,64},{128,160},{160,128},{192,224},{224,1... | collective-permute-start | bytes 2359304 | tf_op jit(solution)/shard_map/ppermute | solution.py:41
  102.9 19.7 %all-to-all-start.3 = ((bf16[32,16,512]{2,1,0:T(8,128)(2,1)}), bf16[32,16,512]{2,1,0:T(8,128)(2,1)}, u32[]{:S(2)}, u32[]{:S(2)}) async-start(bf16[32,16,512]{2,1,0:T(8,128)(2,1)} %bitcast.59), calls=%async_computation.3 | async-start | bytes 1048576 | tf_op jit(solution)/shard_map/all_to_all | solution.py:27
  110.6 2.6 %collective-permute-start.5 = (bf16[4,3,64,512]{3,2,1,0:T(8,128)(2,1)}, bf16[4,3,64,512]{3,2,1,0:T(8,128)(2,1)}, u32[]{:S(2)}, u32[]{:S(2)}) collective-permute-start(bf16[4,3,64,512]{3,2,1,0:T(8,128)(2,1)} %get-tuple-element.95), channel_id=1, source_target_pairs={{0,32},{32,0},{64,96},{96,64},{128,160},{160,128},{192,224},{224,1... | collective-permute-start | bytes 2359304 | tf_op jit(solution)/shard_map/ppermute | solution.py:41
  125.3 17.1 %collective-permute-start.8 = (bf16[384,512]{1,0:T(8,128)(2,1)}, bf16[384,512]{1,0:T(8,128)(2,1)}, u32[]{:S(2)}, u32[]{:S(2)}) collective-permute-start(bf16[384,512]{1,0:T(8,128)(2,1)} %get-tuple-element.115), channel_id=1, source_target_pairs={{0,64},{32,96},{64,128},{96,160},{128,192},{160,224},{192,0},{224,... | collective-permute-start | bytes 1179656 | tf_op jit(solution)/shard_map/ppermute | solution.py:37
  126.9 16.3 %collective-permute-start.9 = (bf16[384,512]{1,0:T(8,128)(2,1)}, bf16[384,512]{1,0:T(8,128)(2,1)}, u32[]{:S(2)}, u32[]{:S(2)}) collective-permute-start(bf16[384,512]{1,0:T(8,128)(2,1)} %get-tuple-element.116), channel_id=1, source_target_pairs={{0,128},{32,160},{64,192},{96,224},{128,0},{160,32},{192,64},{224,... | collective-permute-start | bytes 1179656 | tf_op jit(solution)/shard_map/ppermute | solution.py:37
  129.8 13.4 %collective-permute-start.10 = (bf16[384,512]{1,0:T(8,128)(2,1)}, bf16[384,512]{1,0:T(8,128)(2,1)}, u32[]{:S(2)}, u32[]{:S(2)}) collective-permute-start(bf16[384,512]{1,0:T(8,128)(2,1)} %get-tuple-element.117), channel_id=1, source_target_pairs={{0,192},{32,224},{64,0},{96,32},{128,64},{160,96},{192,128},{224,1... | collective-permute-start | bytes 1179656 | tf_op jit(solution)/shard_map/ppermute | solution.py:37
  131.2 4.6 %collective-permute-start.7 = (bf16[64,512]{1,0:T(8,128)(2,1)}, bf16[64,512]{1,0:T(8,128)(2,1)}, u32[]{:S(2)}, u32[]{:S(2)}) collective-permute-start(bf16[64,512]{1,0:T(8,128)(2,1)} %get-tuple-element.107.grad_own), channel_id=1, source_target_pairs={{1,0},{2,1},{3,2},{4,3},{5,4},{6,5},{7,6},{8,7},{9,8},{10,9},{11,1... | collective-permute-start | bytes 196616 | tf_op jit(solution)/shard_map/ppermute | solution.py:23
  131.2 4.9 %collective-permute-start.6 = (bf16[64,512]{1,0:T(8,128)(2,1)}, bf16[64,512]{1,0:T(8,128)(2,1)}, u32[]{:S(2)}, u32[]{:S(2)}) collective-permute-start(bf16[64,512]{1,0:T(8,128)(2,1)} %get-tuple-element.107.grad_own), channel_id=1, source_target_pairs={{0,1},{1,2},{2,3},{3,4},{4,5},{5,6},{6,7},{7,8},{8,9},{9,10},{10,1... | collective-permute-start | bytes 196616 | tf_op jit(solution)/shard_map/ppermute | solution.py:23
  143.2 2.4 %collective-permute-start.11 = (bf16[512,640]{1,0:T(8,128)(2,1)}, bf16[512,640]{1,0:T(8,128)(2,1)}, u32[]{:S(2)}, u32[]{:S(2)}) collective-permute-start(bf16[512,640]{1,0:T(8,128)(2,1)} %get-tuple-element.119), channel_id=1, source_target_pairs={{0,32},{32,0},{64,96},{96,64},{128,160},{160,128},{192,224},{224,1... | collective-permute-start | bytes 1966088 | tf_op jit(solution)/shard_map/ppermute | solution.py:41
  200.6 17.6 %all-to-all-start.6 = ((bf16[32,16,256]{2,1,0:T(8,128)(2,1)}), bf16[32,16,256]{2,1,0:T(8,128)(2,1)S(1)}, u32[]{:S(2)}, u32[]{:S(2)}) async-start(bf16[32,16,256]{2,1,0:T(8,128)(2,1)} %broadcast_in_dim.2), calls=%async_computation.6 | async-start | bytes 524288 | tf_op jit(solution)/shard_map/all_to_all | solution.py:27

commit v2 on v1

--- a/solution.py
+++ b/solution.py
@@ -268,14 +268,11 @@
         sent[:, place] = jnp.where(first, total[:, 1], total[:, 0]).astype(BF16)
 
 
-def add_cores(chip, last_kept, last_other, first_kept, first_other, *outs):
-    blocks, rows, _ = last_kept.shape
-    pairs = ((last_kept, last_other), (first_kept, first_other))
+def add_cores(chip, kept, other, *outs):
+    blocks = kept.shape[0]
     for step, out in enumerate(outs):
         place = lax.rem(chip[0] + step, blocks)
-        for layer, (kept, other) in enumerate(pairs):
-            total = kept[place].astype(F32) + other[place].astype(F32)
-            out[pl.ds(layer * rows, rows)] = total.astype(BF16)
+        out[...] = (kept[place].astype(F32) + other[place].astype(F32)).astype(BF16)
 
 
 def start_back(upstream, returned, sends, mesh_sum, w_node, gains, start_out, sum_out):
@@ -351,9 +348,11 @@
 def pack(kept, other, *refs):
     blocks, out = refs[:-1], refs[-1]
     rows = blocks[0].shape[0]
-    total = sum(block[...].astype(F32) for block in blocks)
-    out[:, :rows] = total.T.astype(BF16)
-    out[:, rows:] = (kept[...].astype(F32) + other[...].astype(F32)).astype(BF16)
+    per = len(blocks) // 2
+    for place in range(2):
+        total = sum(block[...].astype(F32) for block in blocks[place * per : (place + 1) * per])
+        out[:, pl.ds(place * rows, rows)] = total.T.astype(BF16)
+    out[:, 2 * rows :] = (kept[...].astype(F32) + other[...].astype(F32)).astype(BF16)
 
 
 def sum_blocks(blocks, out):
@@ -454,7 +453,16 @@
             weight_grads, [(shape, BF16)] * 2, [core, *arrays], unit * (pairs + 2 * nodes), scalars=(0,)
         )
         rows = (bands // 2, 3 * width // bands, width)
-        return kept.reshape(rows), to_other_core(sent).reshape(rows)
+        return call(
+            add_cores,
+            [(rows[1:], BF16)] * (bands // 2),
+            [chip, kept.reshape(rows), to_other_core(sent).reshape(rows)],
+            0,
+            scalars=(0,),
+        )
+
+    def over_chips(parts):
+        return [parts[0]] + [along_y(part, step) for step, part in enumerate(parts) if step]
 
     def last_layer(scale, *refs):
         layer_last(scale[0], *refs)
@@ -470,6 +478,7 @@
     returned = exchange(grad_halo.reshape(peers, -1, width), "mesh").reshape(-1, width)
     last_rows = core_halves(last_gathered, last_pair, middle, last_self, last_sum, last_norm)
     returned, last_rows = lax.optimization_barrier((returned, last_rows))
+    last_rows = over_chips(last_rows)
     grad_norm, grad_pair, grad_self, grad_halo, upstream = call(
         layer_first_back,
         back_shapes,
@@ -481,10 +490,7 @@
     first_rows = core_halves(gathered, grad_pair, latent, grad_self, node_sum, grad_norm)
     chips = bands // 2
     shared = 6 * width // bands
-    parts = call(
-        add_cores, [((shared, width), BF16)] * chips, [chip, *last_rows, *first_rows], 0, scalars=(0,)
-    )
-    returned, parts = lax.optimization_barrier((returned, parts))
+    returned, first_rows = lax.optimization_barrier((returned, first_rows))
     grad_start, grad_sum = call(
         start_back,
         [((nodes, width), BF16), ((nodes, width), BF16)],
@@ -493,8 +499,8 @@
         picked={4: 1},
     )
     grad_west, grad_east = from_sides(grad_sum, grad_sum)
-    grad_sum, parts = lax.optimization_barrier((grad_sum, parts))
-    parts = [parts[0]] + [along_y(parts[step], step) for step in range(1, chips)]
+    grad_sum, first_rows, last_rows = lax.optimization_barrier((grad_sum, first_rows, last_rows))
+    parts = last_rows + over_chips(first_rows)
     part = width + EMBED_HALF
     kept, passed = call(
         edge_back,

time: 220 us -> 218 us (level)
  waiting for transfers between devices: 54 us -> 45.6 us
  starting transfers between devices: 42.4 us -> 48.4 us
    ppermute x3 -> x6, starting transfers between devices: 5.83 us -> 11.7 us  [along_y(): lax.ppermute(block, 'grid', [(i, (i + 2 * step) % count) for i in range(c...]
    ppermute x3, waiting for transfers between devices: 7.69 us -> 5.05 us  [to_other_core(): lax.ppermute(block, 'grid', [(i, i ^ 1) for i in range(lax.axis_size('gri...]
    ppermute x3, waiting for transfers between devices: 2.56 us -> 0.01 us  [from_sides(): lax.ppermute(to_west, 'mesh', backward)]
    all_to_all x4, waiting for transfers between devices: 38.2 us -> 35.9 us  [exchange(): return lax.all_to_all(blocks, axis, split_axis=0, concat_axis=0, tiled=True)]
    pallas_call x13 -> x14, Pallas kernels: 45.8 us -> 47.2 us  [call(): pl.pallas_call(kernel, grid=(1,), in_specs=specs, out_specs=[pl.BlockSpec...]
  transfers between devices with their start and end apart: 16 -> 19, of which waited for: 12 -> 8; matrix products, arithmetic and copies ran while one was open for 2% -> 2% of each run, Pallas kernels for 9% -> 11%
where the time goes in v2:
time: 218 us; the launch traced here: 217 us
  blocking collectives  66.4 us (30%)
  starting transfers between devices  48.4 us (22%)
  Pallas kernels  47.2 us (22%)
  waiting for transfers between devices  45.6 us (21%)
  local copies, waits for them, and re-layouts  6.42 us (3%)
    all_to_all x3, blocking collectives, exchange(): return lax.all_to_all(blocks, axis, split_axis=0, concat_axis=0, tiled=True)  66.4 us
    pallas_call x14, Pallas kernels, call(): pl.pallas_call(kernel, grid=(1,), in_specs=specs, out_specs=[pl.BlockSpec...  47.2 us
    all_to_all x4, waiting for transfers between devices, exchange(): return lax.all_to_all(blocks, axis, split_axis=0, concat_axis=0, tiled=True)  35.9 us
    all_to_all x4, starting transfers between devices, exchange(): return lax.all_to_all(blocks, axis, split_axis=0, concat_axis=0, tiled=True)  27.2 us
    ppermute x6, starting transfers between devices, along_y(): lax.ppermute(block, 'grid', [(i, (i + 2 * step) % count) for i in range(c...  11.7 us
    ppermute x3, starting transfers between devices, from_sides(): lax.ppermute(to_west, 'mesh', backward)  7.19 us
    ppermute x3, waiting for transfers between devices, to_other_core(): lax.ppermute(block, 'grid', [(i, i ^ 1) for i in range(lax.axis_size('gri...  5.05 us
    ppermute x3, waiting for transfers between devices, from_sides(): lax.ppermute(to_east, 'mesh', forward)  4.6 us
  transfers between devices with their start and end apart: 19, of which 8 were waited for; matrix products, arithmetic and copies ran while one was open for 2% of the time, Pallas kernels for 11%

profile of v2, /device:TPU:32, one launch (start us, length us, event | category | flops | bytes accessed | tf_op | source)
XLA Modules:
  0.0 216.8 jit_solution(14234388561780960117)
XLA Ops:
  4.6 4.5 %shard_map.147 = (f32[512,512]{1,0:T(8,128)}, bf16[768,512]{1,0:T(8,128)(2,1)}, bf16[768,512]{1,0:T(8,128)(2,1)}, bf16[768,512]{1,0:T(8,128)(2,1)}) custom-call(s32[1,3]{1,0:T(1,128)} %counts.3, bf16[227,512]{1,0:T(8,128)(2,1)} %bitcast.65, s32[3,256]{1,0:T(4,128)} %sources.3, bf16[227,512]{1,0:T(8,128)(2,1)} %w_embed.1, bf16[2,512,512]{2,1,0:T(8,128)(2,1)} %w_edge.3, ...), custom_call_target="tpu_custom_call" | custom-call | flops 1073741824 | bytes 4932620 | tf_op jit(solution)/shard_map/pallas_call | solution.py:118
  9.2 3.5 %collective-permute-done.info_west = f32[2,256]{1,0:T(2,128)} collective-permute-done((f32[2,256]{1,0:T(2,128)}, f32[2,256]{1,0:T(2,128)}, u32[]{:S(2)}, u32[]{:S(2)}) %collective-permute-start) | collective-permute-done | bytes 2080 | tf_op jit(solution)/shard_map/ppermute | solution.py:23
  14.7 5.3 %collective-permute-start.3 = (bf16[64,512]{1,0:T(8,128)(2,1)}, bf16[64,512]{1,0:T(8,128)(2,1)}, u32[]{:S(2)}, u32[]{:S(2)}) collective-permute-start(bf16[64,512]{1,0:T(8,128)(2,1)} %get-tuple-element.81), channel_id=1, source_target_pairs={{1,0},{2,1},{3,2},{4,3},{5,4},{6,5},{7,6},{8,7},{9,8},{10,9},{11,1... | collective-permute-start | bytes 196616 | tf_op jit(solution)/shard_map/ppermute | solution.py:23
  25.1 12.2 %all-to-all-start = ((bf16[32,16,512]{2,1,0:T(8,128)(2,1)}), bf16[32,16,512]{2,1,0:T(8,128)(2,1)}, u32[]{:S(2)}, u32[]{:S(2)}) async-start(bf16[32,16,512]{2,1,0:T(8,128)(2,1)} %bitcast.61), calls=%async_computation | async-start | bytes 1048576 | tf_op jit(solution)/shard_map/all_to_all | solution.py:27
  38.7 13.7 %all-to-all-done = bf16[32,16,512]{2,1,0:T(8,128)(2,1)} async-done(((bf16[32,16,512]{2,1,0:T(8,128)(2,1)}), bf16[32,16,512]{2,1,0:T(8,128)(2,1)}, u32[]{:S(2)}, u32[]{:S(2)}) %all-to-all-start) | async-done | bytes 524320 | tf_op jit(solution)/shard_map/all_to_all | solution.py:27
  52.3 4.1 %shard_map.150 = (bf16[384,512]{1,0:T(8,128)(2,1)}, bf16[6,64,512]{2,1,0:T(8,128)(2,1)}, bf16[64,512]{1,0:T(8,128)(2,1)}, f32[64,512]{1,0:T(8,128)}, bf16[64,512]{1,0:T(8,128)(2,1)}, /*index=5*/bf16[512,512]{1,0:T(8,128)(2,1)}) custom-call(bf16[64,512]{1,0:T(8,128)(2,1)} %get-tuple-element.82.latent, bf16[512,512]{1,0:T(8,128)(2,1)} %bitcast.5.halo, ...), custom_call_target="tpu_custom_call" | custom-call | flops 402653184 | bytes 5320192 | tf_op jit(solution)/shard_map/pallas_call | solution.py:118
  56.4 19.0 %all_to_all.35 = bf16[32,16,512]{2,1,0:T(8,128)(2,1)} all-to-all(bf16[32,16,512]{2,1,0:T(8,128)(2,1)} %bitcast.62), channel_id=1, replica_groups=mesh['grid'=8,'mesh'=32] {'mesh'}, dimensions={0} | all-to-all | bytes 1048576 | tf_op jit(solution)/shard_map/all_to_all | solution.py:27
  75.4 4.7 %shard_map.151 = (bf16[64,512]{1,0:T(8,128)(2,1)}, bf16[384,512]{1,0:T(8,128)(2,1)}, bf16[64,512]{1,0:T(8,128)(2,1)}, bf16[64,512]{1,0:T(8,128)(2,1)}, bf16[384,...) custom-call(f32[1]{0:T(128)} %constant.26.clone.1.scale, ...), custom_call_target="tpu_custom_call" | custom-call | flops 805306368 | bytes 5514756 | tf_op jit(solution)/shard_map/pallas_call | solution.py:118
  80.1 4.8 %all-to-all-start.2 = ((bf16[32,16,512]{2,1,0:T(8,128)(2,1)}), bf16[32,16,512]{2,1,0:T(8,128)(2,1)}, u32[]{:S(2)}, u32[]{:S(2)}) async-start(bf16[32,16,512]{2,1,0:T(8,128)(2,1)} %bitcast.59), calls=%async_computation.2 | async-start | bytes 1048576 | tf_op jit(solution)/shard_map/all_to_all | solution.py:27
  85.0 3.1 %shard_map.152 = (bf16[4,3,64,512]{3,2,1,0:T(8,128)(2,1)}, bf16[4,3,64,512]{3,2,1,0:T(8,128)(2,1)}) custom-call(s32[1]{0:T(128)} %bitcast.9.core, bf16[384,512]{1,0:T(8,128)(2,1)} %get-tuple-element.89.gathered, bf16[384,512]{1,0:T(8,128)(2,1)} %get-tuple-element.90.grad_pair, bf16[64,512]{1,0:T(8,128)(2,1)} %get-tuple-element.84.refs_0_.latent, ...), custom_call_target="tpu_custom_call" | custom-call | flops 268435456 | bytes 2621444 | tf_op jit(solution)/shard_map/pallas_call | solution.py:118
  93.0 5.9 %all-to-all-done.2 = bf16[32,16,512]{2,1,0:T(8,128)(2,1)} async-done(((bf16[32,16,512]{2,1,0:T(8,128)(2,1)}), bf16[32,16,512]{2,1,0:T(8,128)(2,1)}, u32[]{:S(2)}, u32[]{:S(2)}) %all-to-all-start.2) | async-done | bytes 524320 | tf_op jit(solution)/shard_map/all_to_all | solution.py:27
  98.9 4.0 %shard_map.154 = (bf16[64,512]{1,0:T(8,128)(2,1)}, bf16[384,512]{1,0:T(8,128)(2,1)}, bf16[64,512]{1,0:T(8,128)(2,1)}, bf16[512,512]{1,0:T(8,128)(2,1)}, f32[64,512]{1,0:T(8,128)}) custom-call(f32[64,512]{1,0:T(8,128)} %get-tuple-element.87.upstream, bf16[512,512]{1,0:T(8,128)(2,1)} %bitcast.11.returned, s32[1,512]{1,0:T(1,128)} %reshape.88.sends, ...), custom_call_target="tpu_custom_call" | custom-call | flops 603979776 | bytes 5910016 | tf_op jit(solution)/shard_map/pallas_call | solution.py:118
  102.9 4.6 %all-to-all-start.3 = ((bf16[32,16,512]{2,1,0:T(8,128)(2,1)}), bf16[32,16,512]{2,1,0:T(8,128)(2,1)}, u32[]{:S(2)}, u32[]{:S(2)}) async-start(bf16[32,16,512]{2,1,0:T(8,128)(2,1)} %bitcast.60), calls=%async_computation.3 | async-start | bytes 1048576 | tf_op jit(solution)/shard_map/all_to_all | solution.py:27
  107.5 3.0 %shard_map.155 = (bf16[4,3,64,512]{3,2,1,0:T(8,128)(2,1)}, bf16[4,3,64,512]{3,2,1,0:T(8,128)(2,1)}) custom-call(s32[1]{0:T(128)} %bitcast.9.core, bf16[384,512]{1,0:T(8,128)(2,1)} %get-tuple-element.101.gathered, bf16[384,512]{1,0:T(8,128)(2,1)} %get-tuple-element.106.grad_pair, bf16[64,512]{1,0:T(8,128)(2,1)} %get-tuple-element.82.latent, ...), custom_call_target="tpu_custom_call" | custom-call | flops 268435456 | bytes 2621444 | tf_op jit(solution)/shard_map/pallas_call | solution.py:118
  112.1 2.9 %collective-permute-start.8 = (bf16[192,512]{1,0:T(8,128)(2,1)}, bf16[192,512]{1,0:T(8,128)(2,1)}, u32[]{:S(2)}, u32[]{:S(2)}) collective-permute-start(bf16[192,512]{1,0:T(8,128)(2,1)} %get-tuple-element.125), channel_id=1, source_target_pairs={{0,128},{32,160},{64,192},{96,224},{128,0},{160,32},{192,64},{224,... | collective-permute-start | bytes 589832 | tf_op jit(solution)/shard_map/ppermute | solution.py:37
  118.7 6.2 %all-to-all-done.3 = bf16[32,16,512]{2,1,0:T(8,128)(2,1)} async-done(((bf16[32,16,512]{2,1,0:T(8,128)(2,1)}), bf16[32,16,512]{2,1,0:T(8,128)(2,1)}, u32[]{:S(2)}, u32[]{:S(2)}) %all-to-all-start.3) | async-done | bytes 524320 | tf_op jit(solution)/shard_map/all_to_all | solution.py:27
  124.9 2.7 %shard_map.157 = (bf16[64,512]{1,0:T(8,128)(2,1)}, bf16[64,512]{1,0:T(8,128)(2,1)}) custom-call(f32[64,512]{1,0:T(8,128)} %get-tuple-element.104.upstream, bf16[512,512]{1,0:T(8,128)(2,1)} %bitcast.16.returned, s32[1,512]{1,0:T(1,128)} %reshape.88.sends, bf16[64,512]{1,0:T(8,128)(2,1)} %get-tuple-element.117.mesh_sum, bf16[2,512,512]{2,1,0:T(8,128)(2,1)} %w_edge.3, ...), custom_call_target="tpu_custom_call" | custom-call | flops 100663296 | bytes 1910784 | tf_op jit(solution)/shard_map/pallas_call | solution.py:118
  131.3 2.9 %collective-permute-start.12 = (bf16[192,512]{1,0:T(8,128)(2,1)}, bf16[192,512]{1,0:T(8,128)(2,1)}, u32[]{:S(2)}, u32[]{:S(2)}) collective-permute-start(bf16[192,512]{1,0:T(8,128)(2,1)} %get-tuple-element.140), channel_id=1, source_target_pairs={{0,128},{32,160},{64,192},{96,224},{128,0},{160,32},{192,64},{224,... | collective-permute-start | bytes 589832 | tf_op jit(solution)/shard_map/ppermute | solution.py:37
  135.6 6.4 %shard_map.158 = (bf16[512,640]{1,0:T(8,128)(2,1)}, bf16[512,640]{1,0:T(8,128)(2,1)}) custom-call(s32[1,3]{1,0:T(1,128)} %counts.3, s32[1]{0:T(128)} %bitcast.9.core, f32[2,256]{1,0:T(2,128)} %collective-permute-done.info_west, f32[2,256]{1,0:T(2,128)} %get-tuple-element.168.info_own, f32[2,256]{1,0:T(2,128)} %collective-permute-done.1.info_east, ...), custom_call_target="tpu_custom_call" | custom-call | flops 1610612736 | bytes 5558288 | tf_op jit(solution)/shard_map/pallas_call | solution.py:118
  144.5 3.3 %shard_map.159 = bf16[512,1024]{1,0:T(8,128)(2,1)} custom-call(bf16[512,640]{1,0:T(8,128)(2,1)} %get-tuple-element.142.kept, bf16[512,640]{1,0:T(8,128)(2,1)} %collective-permute-done.14.other, bf16[192,512]{1,0:T(8,128)(2,1)} %get-tuple-element.144.refs_0_, bf16[192,512]{1,0:T(8,128)(2,1)} %collective-permute-done.7.refs_1_, ...), custom_call_target="tpu_custom_call" | custom-call | bytes 3932160 | tf_op jit(solution)/shard_map/pallas_call | solution.py:118
  147.8 35.9 %all_to_all.36.blocks = bf16[32,16,1024]{2,1,0:T(8,128)(2,1)} all-to-all(bf16[32,16,1024]{2,1,0:T(8,128)(2,1)} %bitcast.53), channel_id=1, replica_groups=mesh['grid'=8,'mesh'=32] {'mesh'}, dimensions={0} | all-to-all | bytes 2097152 | tf_op jit(solution)/shard_map/all_to_all | solution.py:27
  185.8 11.4 %all_to_all.37 = bf16[8,16,1024]{2,1,0:T(8,128)(2,1)S(1)} all-to-all(bf16[8,16,1024]{2,1,0:T(8,128)(2,1)} %shard_map.160), channel_id=1, replica_groups=mesh['grid'=8,'mesh'=32] {'grid'}, dimensions={0} | all-to-all | bytes 524288 | tf_op jit(solution)/shard_map/all_to_all | solution.py:27
  198.2 5.6 %all-to-all-start.6 = ((bf16[32,16,256]{2,1,0:T(8,128)(2,1)}), bf16[32,16,256]{2,1,0:T(8,128)(2,1)S(1)}, u32[]{:S(2)}, u32[]{:S(2)}) async-start(bf16[32,16,256]{2,1,0:T(8,128)(2,1)} %broadcast_in_dim.2), calls=%async_computation.6 | async-start | bytes 524288 | tf_op jit(solution)/shard_map/all_to_all | solution.py:27
  205.7 10.1 %all-to-all-done.6 = bf16[32,16,256]{2,1,0:T(8,128)(2,1)S(1)} async-done(((bf16[32,16,256]{2,1,0:T(8,128)(2,1)}), bf16[32,16,256]{2,1,0:T(8,128)(2,1)S(1)}, u32[]{:S(2)}, u32[]{:S(2)}) %all-to-all-start.6) | async-done | bytes 262176 | tf_op jit(solution)/shard_map/all_to_all | solution.py:27
  (54 shorter events, 36.1 us)
Async XLA Ops:
  2.6 6.6 %collective-permute-start.1 = (f32[2,256]{1,0:T(2,128)}, f32[2,256]{1,0:T(2,128)}, u32[]{:S(2)}, u32[]{:S(2)}) collective-permute-start(f32[2,256]{1,0:T(2,128)} %get-tuple-element.166), channel_id=1, source_target_pairs={{1,0},{2,1},{3,2},{4,3},{5,4},{6,5},{7,6},{8,7},{9,8},{10,9},{11,1... | collective-permute-start | bytes 6152 | tf_op jit(solution)/shard_map/ppermute | solution.py:23
  4.5 8.2 %collective-permute-start = (f32[2,256]{1,0:T(2,128)}, f32[2,256]{1,0:T(2,128)}, u32[]{:S(2)}, u32[]{:S(2)}) collective-permute-start(f32[2,256]{1,0:T(2,128)} %get-tuple-element.167), channel_id=1, source_target_pairs={{0,1},{1,2},{2,3},{3,4},{4,5},{5,6},{6,7},{7,8},{8,9},{9,10},{10,1... | collective-permute-start | bytes 6152 | tf_op jit(solution)/shard_map/ppermute | solution.py:23
  14.7 7.9 %collective-permute-start.2 = (bf16[64,512]{1,0:T(8,128)(2,1)}, bf16[64,512]{1,0:T(8,128)(2,1)}, u32[]{:S(2)}, u32[]{:S(2)}) collective-permute-start(bf16[64,512]{1,0:T(8,128)(2,1)} %get-tuple-element.80), channel_id=1, source_target_pairs={{0,1},{1,2},{2,3},{3,4},{4,5},{5,6},{6,7},{7,8},{8,9},{9,10},{10,1... | collective-permute-start | bytes 196616 | tf_op jit(solution)/shard_map/ppermute | solution.py:23
  14.7 7.9 %collective-permute-start.3 = (bf16[64,512]{1,0:T(8,128)(2,1)}, bf16[64,512]{1,0:T(8,128)(2,1)}, u32[]{:S(2)}, u32[]{:S(2)}) collective-permute-start(bf16[64,512]{1,0:T(8,128)(2,1)} %get-tuple-element.81), channel_id=1, source_target_pairs={{1,0},{2,1},{3,2},{4,3},{5,4},{6,5},{7,6},{8,7},{9,8},{10,9},{11,1... | collective-permute-start | bytes 196616 | tf_op jit(solution)/shard_map/ppermute | solution.py:23
  25.1 27.2 %all-to-all-start = ((bf16[32,16,512]{2,1,0:T(8,128)(2,1)}), bf16[32,16,512]{2,1,0:T(8,128)(2,1)}, u32[]{:S(2)}, u32[]{:S(2)}) async-start(bf16[32,16,512]{2,1,0:T(8,128)(2,1)} %bitcast.61), calls=%async_computation | async-start | bytes 1048576 | tf_op jit(solution)/shard_map/all_to_all | solution.py:27
  80.1 18.7 %all-to-all-start.2 = ((bf16[32,16,512]{2,1,0:T(8,128)(2,1)}), bf16[32,16,512]{2,1,0:T(8,128)(2,1)}, u32[]{:S(2)}, u32[]{:S(2)}) async-start(bf16[32,16,512]{2,1,0:T(8,128)(2,1)} %bitcast.59), calls=%async_computation.2 | async-start | bytes 1048576 | tf_op jit(solution)/shard_map/all_to_all | solution.py:27
  88.0 2.6 %collective-permute-start.4 = (bf16[4,3,64,512]{3,2,1,0:T(8,128)(2,1)}, bf16[4,3,64,512]{3,2,1,0:T(8,128)(2,1)}, u32[]{:S(2)}, u32[]{:S(2)}) collective-permute-start(bf16[4,3,64,512]{3,2,1,0:T(8,128)(2,1)} %get-tuple-element.95), channel_id=1, source_target_pairs={{0,32},{32,0},{64,96},{96,64},{128,160},{160,128},{192,224},{224,1... | collective-permute-start | bytes 2359304 | tf_op jit(solution)/shard_map/ppermute | solution.py:41
  102.9 22.0 %all-to-all-start.3 = ((bf16[32,16,512]{2,1,0:T(8,128)(2,1)}), bf16[32,16,512]{2,1,0:T(8,128)(2,1)}, u32[]{:S(2)}, u32[]{:S(2)}) async-start(bf16[32,16,512]{2,1,0:T(8,128)(2,1)} %bitcast.60), calls=%async_computation.3 | async-start | bytes 1048576 | tf_op jit(solution)/shard_map/all_to_all | solution.py:27
  110.5 5.8 %collective-permute-start.5 = (bf16[4,3,64,512]{3,2,1,0:T(8,128)(2,1)}, bf16[4,3,64,512]{3,2,1,0:T(8,128)(2,1)}, u32[]{:S(2)}, u32[]{:S(2)}) collective-permute-start(bf16[4,3,64,512]{3,2,1,0:T(8,128)(2,1)} %get-tuple-element.111), channel_id=1, source_target_pairs={{0,32},{32,0},{64,96},{96,64},{128,160},{160,128},{192,224},{224,1... | collective-permute-start | bytes 2359304 | tf_op jit(solution)/shard_map/ppermute | solution.py:41
  110.5 19.1 %collective-permute-start.7 = (bf16[192,512]{1,0:T(8,128)(2,1)}, bf16[192,512]{1,0:T(8,128)(2,1)}, u32[]{:S(2)}, u32[]{:S(2)}) collective-permute-start(bf16[192,512]{1,0:T(8,128)(2,1)} %get-tuple-element.124), channel_id=1, source_target_pairs={{0,64},{32,96},{64,128},{96,160},{128,192},{160,224},{192,0},{224,... | collective-permute-start | bytes 589832 | tf_op jit(solution)/shard_map/ppermute | solution.py:37
  112.1 17.5 %collective-permute-start.8 = (bf16[192,512]{1,0:T(8,128)(2,1)}, bf16[192,512]{1,0:T(8,128)(2,1)}, u32[]{:S(2)}, u32[]{:S(2)}) collective-permute-start(bf16[192,512]{1,0:T(8,128)(2,1)} %get-tuple-element.125), channel_id=1, source_target_pairs={{0,128},{32,160},{64,192},{96,224},{128,0},{160,32},{192,64},{224,... | collective-permute-start | bytes 589832 | tf_op jit(solution)/shard_map/ppermute | solution.py:37
  115.0 14.6 %collective-permute-start.9 = (bf16[192,512]{1,0:T(8,128)(2,1)}, bf16[192,512]{1,0:T(8,128)(2,1)}, u32[]{:S(2)}, u32[]{:S(2)}) collective-permute-start(bf16[192,512]{1,0:T(8,128)(2,1)} %get-tuple-element.126), channel_id=1, source_target_pairs={{0,192},{32,224},{64,0},{96,32},{128,64},{160,96},{192,128},{224,1... | collective-permute-start | bytes 589832 | tf_op jit(solution)/shard_map/ppermute | solution.py:37
  127.6 7.9 %collective-permute-start.10 = (bf16[64,512]{1,0:T(8,128)(2,1)}, bf16[64,512]{1,0:T(8,128)(2,1)}, u32[]{:S(2)}, u32[]{:S(2)}) collective-permute-start(bf16[64,512]{1,0:T(8,128)(2,1)} %get-tuple-element.127.grad_own), channel_id=1, source_target_pairs={{1,0},{2,1},{3,2},{4,3},{5,4},{6,5},{7,6},{8,7},{9,8},{10,9},{11,1... | collective-permute-start | bytes 196616 | tf_op jit(solution)/shard_map/ppermute | solution.py:23
  127.6 7.9 %collective-permute-start.6 = (bf16[64,512]{1,0:T(8,128)(2,1)}, bf16[64,512]{1,0:T(8,128)(2,1)}, u32[]{:S(2)}, u32[]{:S(2)}) collective-permute-start(bf16[64,512]{1,0:T(8,128)(2,1)} %get-tuple-element.127.grad_own), channel_id=1, source_target_pairs={{0,1},{1,2},{2,3},{3,4},{4,5},{5,6},{6,7},{7,8},{8,9},{9,10},{10,1... | collective-permute-start | bytes 196616 | tf_op jit(solution)/shard_map/ppermute | solution.py:23
  129.6 12.3 %collective-permute-start.11 = (bf16[192,512]{1,0:T(8,128)(2,1)}, bf16[192,512]{1,0:T(8,128)(2,1)}, u32[]{:S(2)}, u32[]{:S(2)}) collective-permute-start(bf16[192,512]{1,0:T(8,128)(2,1)} %get-tuple-element.139), channel_id=1, source_target_pairs={{0,64},{32,96},{64,128},{96,160},{128,192},{160,224},{192,0},{224,... | collective-permute-start | bytes 589832 | tf_op jit(solution)/shard_map/ppermute | solution.py:37
  131.3 10.7 %collective-permute-start.12 = (bf16[192,512]{1,0:T(8,128)(2,1)}, bf16[192,512]{1,0:T(8,128)(2,1)}, u32[]{:S(2)}, u32[]{:S(2)}) collective-permute-start(bf16[192,512]{1,0:T(8,128)(2,1)} %get-tuple-element.140), channel_id=1, source_target_pairs={{0,128},{32,160},{64,192},{96,224},{128,0},{160,32},{192,64},{224,... | collective-permute-start | bytes 589832 | tf_op jit(solution)/shard_map/ppermute | solution.py:37
  134.2 7.8 %collective-permute-start.13 = (bf16[192,512]{1,0:T(8,128)(2,1)}, bf16[192,512]{1,0:T(8,128)(2,1)}, u32[]{:S(2)}, u32[]{:S(2)}) collective-permute-start(bf16[192,512]{1,0:T(8,128)(2,1)} %get-tuple-element.141), channel_id=1, source_target_pairs={{0,192},{32,224},{64,0},{96,32},{128,64},{160,96},{192,128},{224,1... | collective-permute-start | bytes 589832 | tf_op jit(solution)/shard_map/ppermute | solution.py:37
  142.0 2.5 %collective-permute-start.14 = (bf16[512,640]{1,0:T(8,128)(2,1)}, bf16[512,640]{1,0:T(8,128)(2,1)}, u32[]{:S(2)}, u32[]{:S(2)}) collective-permute-start(bf16[512,640]{1,0:T(8,128)(2,1)} %get-tuple-element.143), channel_id=1, source_target_pairs={{0,32},{32,0},{64,96},{96,64},{128,160},{160,128},{192,224},{224,1... | collective-permute-start | bytes 1966088 | tf_op jit(solution)/shard_map/ppermute | solution.py:41
  198.2 17.6 %all-to-all-start.6 = ((bf16[32,16,256]{2,1,0:T(8,128)(2,1)}), bf16[32,16,256]{2,1,0:T(8,128)(2,1)S(1)}, u32[]{:S(2)}, u32[]{:S(2)}) async-start(bf16[32,16,256]{2,1,0:T(8,128)(2,1)} %broadcast_in_dim.2), calls=%async_computation.6 | async-start | bytes 524288 | tf_op jit(solution)/shard_map/all_to_all | solution.py:27
